TPU v7x, 32 devices: a whole 2x2x4 slice. The times are simulated.
32 devices in a mesh: cube: 32 (over z, y, x, core).
Axes of the slice: x: 2, y: 2, z: 4, core: 2. Of those that a mesh axis runs over, the one named last changes fastest.
Arguments:
- vectors: bfloat16 [131072, 768], P('cube'), may hold values from -40 to 40
- child_labels: int32 [2, 131072], P(None, 'cube'), may hold values from 0 to 1, as said below
Outputs:
- held: bfloat16 [229376, 768], P('cube')
- margin_one: float32 [196608], P('cube')
- margin_two: float32 [229376], P('cube')
- centroids: float32 [6, 768], replicated
Inputs may be any that keep to these rules, and one draw needn't show every extreme that they name: `child_labels`: per device, the vectors leaving at the first level number from 1024 to 2048, and 2048 on some device in every draw. `child_labels`: per device, the second-level leavers among its vectors that stay at the first level number at most 512, and among the vectors it sends away at the first level at most 512; in every draw some device holds 512 second-level leavers of each kind (its own stayers and those received at the first level), so its second-level send buffer is full.
All inputs are finite; a program needn't handle non-finite values.
Results may differ from a plain program's by a relative error of at most 0.0011.
Values may be sent and summed in bfloat16 or wider, within the bound.
No kernel may reach another device: no remote copies, remote signals or barrier semaphores. Data moves between devices by JAX's collectives and lax.ppermute only.
A program may use at most 128 MiB of HBM per device.

v0:
```python
import functools
import jax
import jax.numpy as jnp
from jax import lax
from jax.experimental import pallas as pl
from jax.experimental.pallas import tpu as pltpu
from jax.sharding import PartitionSpec as P

BF = jnp.bfloat16
F32 = jnp.float32
I32 = jnp.int32
BLK = 256
HANDS = 8
VMEM_BYTES = 48 * 1024 * 1024


def swap(x, bits):
    return lax.ppermute(x, "cube", [(i, i ^ bits) for i in range(lax.axis_size("cube"))])


def dot(a, b):
    return lax.dot_general(a, b, (((1,), (0,)), ((), ())), preferred_element_type=F32)


def dot_t(a, b):
    return lax.dot_general(a, b, (((1,), (1,)), ((), ())), preferred_element_type=F32)


def iota(shape, dim):
    return lax.broadcasted_iota(I32, shape, dim)


def as_bf(mask):
    return jnp.where(mask, jnp.float32(1), jnp.float32(0)).astype(BF)


def pack(sums, counts, width):
    high = sums.astype(BF).astype(F32)
    middle = (sums - high).astype(BF).astype(F32)
    low = sums - high - middle
    spare = width - 128 * len(counts)
    counts = jnp.concatenate(counts + ([jnp.zeros((1, spare), I32)] if spare else []), axis=1)
    upper, lower = (counts >> 8).astype(F32), (counts & 255).astype(F32)
    return jnp.concatenate([high, middle, low, upper, lower, jnp.zeros((2, width), F32)], axis=0).astype(BF)


def unpack(extra):
    extra = extra.astype(F32)
    sums = extra[0:4] + extra[4:8] + extra[8:12]
    return sums, extra[12:13] * 256.0 + extra[13:14]


def count_at(extra, k):
    extra = extra[12:14, 128 * k : 128 * k + 1].astype(F32)
    return (extra[0:1] * 256.0 + extra[1:2]).astype(I32)


def spec(memory):
    return pl.BlockSpec(memory_space=memory)


def params():
    return pltpu.CompilerParams(vmem_limit_bytes=VMEM_BYTES)


def plan_kernel(here, labels, pos, off_ref, every, leavers):
    rows = labels.shape[1]
    blocks = rows // BLK
    leave = labels[0:1, :] != here[0]
    miss = labels[1:2, :] != here[1]
    code = jnp.where(leave, jnp.where(miss, 0, 1), jnp.where(miss, 2, 3))
    code = jnp.concatenate(
        [jnp.broadcast_to(code[:, b * BLK : (b + 1) * BLK], (8, BLK)) for b in range(blocks)], axis=0
    )
    tall = 8 * blocks
    kind = iota((tall, BLK), 0) & 7
    mask = (code == kind) | ((kind == 4) & (code <= 1))
    maskb = as_bf(mask)
    upper = as_bf(iota((BLK, BLK), 0) <= iota((BLK, BLK), 1))
    before = dot(maskb, upper)
    total = dot(maskb, jnp.ones((BLK, BLK), BF)).astype(BF)
    r, c = iota((tall, tall), 0), iota((tall, tall), 1)
    same = ((r ^ c) & 7) == 0
    earlier = as_bf((same & (c < r)) | (((r & 7) == 1) & ((c & 7) == 0)))
    off = dot(earlier, total)
    pos[...] = jnp.where(mask, (before + off).astype(I32) - 1, -1)
    off_ref[...] = off[:, :128].astype(I32)
    r8, c8 = iota((8, tall), 0), iota((8, tall), 1)
    count = dot(as_bf(r8 == (c8 & 7)), total)[:, :128].astype(I32)
    every[...] = count
    leavers[...] = jnp.broadcast_to(count[4:5], leavers.shape)


def plan_call(here, labels):
    rows = labels.shape[1]
    tall = 8 * rows // BLK
    return pl.pallas_call(
        plan_kernel,
        out_shape=[
            jax.ShapeDtypeStruct((tall, BLK), I32),
            jax.ShapeDtypeStruct((tall, 128), I32),
            jax.ShapeDtypeStruct((8, 128), I32),
            jax.ShapeDtypeStruct((8, 128), I32),
        ],
        in_specs=[spec(pltpu.SMEM), spec(pltpu.VMEM)],
        out_specs=[spec(pltpu.VMEM)] * 4,
        compiler_params=params(),
        cost_estimate=pl.CostEstimate(flops=10**8, bytes_accessed=10**5, transcendentals=0),
        name="plan_places",
    )(here, labels)


def sort_kernel(here, labels, pos_ref, off_ref, every, x_hbm, first, middle, rest, x, buf, tail, sem_in, sem_out):
    rows = labels.shape[1]
    blocks = rows // BLK
    cap = rows // 2
    step = rows // 4
    loads = [
        pltpu.make_async_copy(x_hbm.at[pl.ds(k * step, step)], x.at[pl.ds(k * step, step)], sem_in.at[k])
        for k in range(4)
    ]
    for load in loads:
        load.start()
    buf[...] = jnp.zeros_like(buf)
    group = 2 * labels[0:1, :] + labels[1:2, :]
    wide = BLK + 16
    slot = iota((wide, BLK), 0)
    sums = jnp.zeros((4, x.shape[1]), F32)
    for b in range(blocks):
        if b % (step // BLK) == 0:
            loads[b // (step // BLK)].wait()
        hot = []
        bases = []
        for kind in (0, 1):
            base = off_ref[8 * b + kind : 8 * b + kind + 1, 0:1]
            base = jnp.minimum((base[0, 0] // 16) * 16, cap)
            place = pos_ref[8 * b + kind : 8 * b + kind + 1, :]
            hot.append(as_bf(slot == place - base))
            bases.append(pl.multiple_of(base, 16))
        hot.append(as_bf((iota((16, BLK), 0) & 3) == group[:, b * BLK : (b + 1) * BLK]))
        got = dot(jnp.concatenate(hot, axis=0), x[b * BLK : (b + 1) * BLK, :])
        for kind in (0, 1):
            buf[pl.ds(bases[kind], wide), :] += got[kind * wide : (kind + 1) * wide].astype(BF)
        sums += got[2 * wide : 2 * wide + 4]
    one, two = here[0], here[1]
    kinds = [every[k : k + 1] for k in range(4)]
    counts = []
    for g in range(4):
        away, miss = jnp.int32(g >> 1) != one, jnp.int32(g & 1) != two
        counts.append(jnp.where(away, jnp.where(miss, kinds[0], kinds[1]), jnp.where(miss, kinds[2], kinds[3])))
    tail[...] = pack(sums, counts + [kinds[0], kinds[2]], x.shape[1])
    part = cap // 4
    stores = [
        pltpu.make_async_copy(buf.at[pl.ds(0, part)], first.at[pl.ds(0, part)], sem_out.at[0]),
        pltpu.make_async_copy(buf.at[pl.ds(part, part)], middle, sem_out.at[1]),
        pltpu.make_async_copy(buf.at[pl.ds(2 * part, 2 * part)], rest, sem_out.at[2]),
        pltpu.make_async_copy(tail, first.at[pl.ds(part, 16)], sem_out.at[3]),
    ]
    for store in stores:
        store.start()
    for store in stores:
        store.wait()


def sort_call(here, labels, pos, off, every, vectors):
    rows, width = vectors.shape
    part = rows // 8
    return pl.pallas_call(
        sort_kernel,
        out_shape=[
            jax.ShapeDtypeStruct((part + 16, width), BF),
            jax.ShapeDtypeStruct((part, width), BF),
            jax.ShapeDtypeStruct((2 * part, width), BF),
        ],
        in_specs=[spec(pltpu.SMEM)] + [spec(pltpu.VMEM)] * 4 + [spec(pl.ANY)],
        out_specs=[spec(pl.ANY), spec(pltpu.HBM), spec(pl.ANY)],
        scratch_shapes=[
            pltpu.VMEM((rows, width), BF),
            pltpu.VMEM((rows // 2 + BLK + 16, width), BF),
            pltpu.VMEM((16, width), BF),
            pltpu.SemaphoreType.DMA((4,)),
            pltpu.SemaphoreType.DMA((4,)),
        ],
        compiler_params=params(),
        cost_estimate=pl.CostEstimate(flops=8 * 10**9, bytes_accessed=10 * 10**6, transcendentals=0),
        name="sort_leavers",
    )(here, labels, pos, off, every, vectors)


def deal_kernel(rest, own, near, top, far, *refs):
    hands, (tail, sem) = refs[:HANDS], refs[HANDS:]
    rows, width = rest.shape
    turns = rows // 16 // HANDS
    counts = jnp.concatenate([ref[0:1, :] for ref in (own, near, top, far)], axis=1)
    counts = jnp.concatenate([counts, jnp.zeros((1, width - 512), I32)], axis=1)
    upper, lower = (counts >> 8).astype(F32), (counts & 255).astype(F32)
    tail[...] = jnp.concatenate([upper, lower, jnp.zeros((14, width), F32)], axis=0).astype(BF)
    copies = []
    for h, hand in enumerate(hands):
        for turn in range(turns):
            block = rest.at[pl.ds(16 * (h + HANDS * turn), 16)]
            copies.append(pltpu.make_async_copy(block, hand.at[pl.ds(16 * turn, 16)], sem.at[h, turn]))
        copies.append(pltpu.make_async_copy(tail, hand.at[pl.ds(16 * turns, 16)], sem.at[h, turns]))
    for copy in copies:
        copy.start()
    for copy in copies:
        copy.wait()


def deal_call(rest, *counts):
    rows, width = rest.shape
    turns = rows // 16 // HANDS
    return pl.pallas_call(
        deal_kernel,
        out_shape=[jax.ShapeDtypeStruct((16 * turns + 16, width), BF)] * HANDS,
        in_specs=[spec(pl.ANY)] + [spec(pltpu.VMEM)] * 4,
        out_specs=[spec(pl.ANY)] * HANDS,
        scratch_shapes=[pltpu.VMEM((16, width), BF), pltpu.SemaphoreType.DMA((HANDS, turns + 1))],
        compiler_params=params(),
        cost_estimate=pl.CostEstimate(flops=0, bytes_accessed=3 * 10**6, transcendentals=0),
        name="deal_rest",
    )(rest, *counts)


def pack_kernel(step, *refs):
    hands, (out, longest, begins) = refs[:HANDS], refs[HANDS:]
    rows = hands[0].shape[0] - 16
    out[...] = jnp.zeros_like(out)
    full = []
    for hand in hands:
        count = hand[rows : rows + 2, 0:512].astype(F32)
        count = (count[0:1] * 256.0 + count[1:2]).astype(I32)
        full.append((jnp.maximum(count - rows * HANDS, 0) + 15) >> 4)
    place = jnp.zeros((1, 512), I32)
    for h, hand in enumerate(hands):
        base = pl.multiple_of(place[0, 0] * 16, 16)
        out[pl.ds(base, rows), :] = hand[0:rows, :]
        begins[h : h + 1, :] = place[:, 256:384] * 16
        place = jnp.minimum(place + ((full[h] + (HANDS - 1 - h)) >> 3), (h + 1) * (rows // 16))
    most = jnp.zeros((1, 512), I32)
    for other in range(HANDS):
        size = jnp.zeros((1, 512), I32)
        for h in range(HANDS):
            size = size + ((full[other ^ h] + (HANDS - 1 - h)) >> 3)
        most = jnp.maximum(most, size)
    most = jnp.max(most.astype(F32), axis=1, keepdims=True).astype(I32)
    per = step // 16
    longest[...] = jnp.broadcast_to(jnp.minimum(most + per - 1, out.shape[0] // 16) // per, longest.shape)


def pack_call(step, hands):
    rows, width = hands[0].shape
    rows -= 16
    return pl.pallas_call(
        functools.partial(pack_kernel, step),
        out_shape=[
            jax.ShapeDtypeStruct((rows * HANDS, width), BF),
            jax.ShapeDtypeStruct((8, 128), I32),
            jax.ShapeDtypeStruct((8, 128), I32),
        ],
        in_specs=[spec(pltpu.VMEM)] * HANDS,
        out_specs=[spec(pltpu.VMEM)] * 3,
        compiler_params=params(),
        cost_estimate=pl.CostEstimate(flops=0, bytes_accessed=3 * 10**6, transcendentals=0),
        name="pack_hands",
    )(*hands)


def part_kernel(begins, pack_in, *refs):
    hands, sem = refs[:HANDS], refs[HANDS]
    rows = hands[0].shape[0]
    copies = []
    for h, hand in enumerate(hands):
        base = pl.multiple_of((begins[h, 0] // 16) * 16, 16)
        copies.append(pltpu.make_async_copy(pack_in.at[pl.ds(base, rows)], hand, sem.at[h]))
    for copy in copies:
        copy.start()
    for copy in copies:
        copy.wait()


def part_call(begins, pack_in):
    rows, width = pack_in.shape
    return pl.pallas_call(
        part_kernel,
        out_shape=[jax.ShapeDtypeStruct((rows // HANDS, width), BF)] * HANDS,
        in_specs=[spec(pltpu.SMEM), spec(pl.ANY)],
        out_specs=[spec(pl.ANY)] * HANDS,
        scratch_shapes=[pltpu.SemaphoreType.DMA((HANDS,))],
        compiler_params=params(),
        cost_estimate=pl.CostEstimate(flops=0, bytes_accessed=3 * 10**6, transcendentals=0),
        name="part_pack",
    )(begins, pack_in)


def second_send_kernel(off, pos, extra, x_ref, second, meta, buf, ranks):
    step = pl.program_id(0)

    @pl.when(step == 0)
    def _():
        buf[...] = jnp.zeros_like(buf)
        ranks[...] = jnp.zeros_like(ranks)

    half = second.shape[0] - 16
    cap = 4 * half
    wide = BLK + 16
    blocks = x_ref.shape[0] // BLK
    line = iota((16, BLK), 0)
    for sub in range(blocks):
        b = step * blocks + sub
        place = pos[8 * sub : 8 * sub + 8, :]
        base = jnp.minimum((off[8 * b + 2, 0] // 16) * 16, half)
        hot = as_bf(iota((wide, BLK), 0) == place[2:3, :] - base)
        got = dot(hot, x_ref[sub * BLK : (sub + 1) * BLK, :])
        buf[pl.ds(pl.multiple_of(base, 16), wide), :] += got.astype(BF)
        rank = place[4:5, :]
        value = jnp.where(line == 0, rank >> 8, jnp.where(line == 1, rank & 255, 1))
        value = jnp.where(rank >= 0, value, 0).astype(F32).astype(BF)
        for kind in (0, 1):
            base = pl.multiple_of(jnp.minimum((off[8 * b + kind, 0] // 128) * 128, cap), 128)
            hot = as_bf(iota((BLK + 128, BLK), 0) == place[kind : kind + 1, :] - base)
            ranks[:, pl.ds(base, BLK + 128)] += dot_t(value, hot)[:8]

    @pl.when(step == pl.num_programs(0) - 1)
    def _():
        second[0:half, :] = buf[0:half, :]
        second[half:, :] = extra[...]
        seen = ranks[2:3, :cap] > 0.5
        rank = (ranks[0:1, :cap] * 256.0 + ranks[1:2, :cap]).astype(I32)
        goal = jnp.where(seen, rank, 1 << 20)
        line = cap // 8
        for k in range(8):
            meta[k : k + 1, :] = goal[:, k * line : (k + 1) * line]


def second_send_call(off, pos, first, vectors):
    rows, width = vectors.shape
    cap = rows // 2
    half = rows // 8
    return pl.pallas_call(
        second_send_kernel,
        grid=(rows // 1024,),
        out_shape=[
            jax.ShapeDtypeStruct((half + 16, width), BF),
            jax.ShapeDtypeStruct((8, cap // 8), I32),
        ],
        in_specs=[
            spec(pltpu.SMEM),
            pl.BlockSpec((8 * 1024 // BLK, BLK), lambda b: (b, 0)),
            pl.BlockSpec((16, width), lambda b: (half // 16, 0)),
            pl.BlockSpec((1024, width), lambda b: (b, 0)),
        ],
        out_specs=[
            pl.BlockSpec((half + 16, width), lambda b: (0, 0)),
            pl.BlockSpec((8, cap // 8), lambda b: (0, 0)),
        ],
        scratch_shapes=[pltpu.VMEM((half + BLK + 16, width), BF), pltpu.VMEM((8, cap + BLK + 128), F32)],
        compiler_params=params(),
        cost_estimate=pl.CostEstimate(flops=6 * 10**9, bytes_accessed=8 * 10**6, transcendentals=0),
        name="second_send",
    )(off, pos, first, vectors)


def own_kernel(pos, x_ref, held):
    same = iota((BLK, BLK), 0) == iota((BLK, BLK), 1)
    for sub in range(x_ref.shape[0] // BLK):
        lines = slice(sub * BLK, (sub + 1) * BLK)
        held[lines, :] = dot(as_bf(same & (pos[8 * sub + 3 : 8 * sub + 4, :] >= 0)), x_ref[lines, :]).astype(BF)


def own_call(pos, vectors):
    rows, width = vectors.shape
    return pl.pallas_call(
        own_kernel,
        grid=(rows // 1024,),
        out_shape=jax.ShapeDtypeStruct((rows + rows // 2 + rows // 4, width), BF),
        in_specs=[
            pl.BlockSpec((8 * 1024 // BLK, BLK), lambda b: (b, 0)),
            pl.BlockSpec((1024, width), lambda b: (b, 0)),
        ],
        out_specs=pl.BlockSpec((1024, width), lambda b: (b, 0)),
        compiler_params=params(),
        cost_estimate=pl.CostEstimate(flops=2 * 10**9, bytes_accessed=13 * 10**6, transcendentals=0),
        name="own_slots",
    )(pos, vectors)


def margins(score, shift, first, width):
    return (score[first + 1 : first + 2] - score[first : first + 1] - shift) / width


def put_lines(ref, start, values):
    for k in range(values.shape[1] // 128):
        ref[start + k : start + k + 1, :] = values[:, 128 * k : 128 * (k + 1)]


def centre_kernel(here, total, labels, x_ref, cents, centres, shifts, one, two):
    width = x_ref.shape[1]

    @pl.when(pl.program_id(0) == 0)
    def _():
        sums, counts = total[0:4, :], total[4:8, :]
        low = (sums[0:1] + sums[1:2]) / (counts[0:1] + counts[1:2])
        high = (sums[2:3] + sums[3:4]) / (counts[2:3] + counts[3:4])
        groups = sums / counts
        cents[0:1, :] = low
        cents[1:2, :] = high
        cents[2:6, :] = groups
        top = here[0] == 1
        left = jnp.where(top, groups[2:3], groups[0:1])
        right = jnp.where(top, groups[3:4], groups[1:2])
        centres[...] = jnp.concatenate([low, high, left, right, jnp.zeros((12, width), F32)], axis=0).astype(BF)
        for k, (a, b) in enumerate(((low, high), (left, right))):
            shift = 0.5 * (jnp.sum(b * b, axis=1, keepdims=True) - jnp.sum(a * a, axis=1, keepdims=True))
            shifts[k : k + 1, :] = jnp.broadcast_to(shift, (1, 128))

    score = dot_t(centres[...], x_ref[...])
    stay = labels[0:1, :] == here[0]
    keep = stay & (labels[1:2, :] == here[1])
    put_lines(one, 0, jnp.where(stay, margins(score, shifts[0:1, 0:1], 0, width), 0.0))
    put_lines(two, 0, jnp.where(keep, margins(score, shifts[1:2, 0:1], 2, width), 0.0))


def centre_call(here, total, labels, vectors):
    rows, width = vectors.shape
    cap = rows // 2
    return pl.pallas_call(
        centre_kernel,
        grid=(rows // 1024,),
        out_shape=[
            jax.ShapeDtypeStruct((6, width), F32),
            jax.ShapeDtypeStruct((16, width), BF),
            jax.ShapeDtypeStruct((8, 128), F32),
            jax.ShapeDtypeStruct(((rows + cap) // 128, 128), F32),
            jax.ShapeDtypeStruct(((rows + cap + cap // 2) // 128, 128), F32),
        ],
        in_specs=[
            spec(pltpu.SMEM),
            pl.BlockSpec((8, width), lambda b: (0, 0)),
            pl.BlockSpec((2, 1024), lambda b: (0, b)),
            pl.BlockSpec((1024, width), lambda b: (b, 0)),
        ],
        out_specs=[
            pl.BlockSpec((6, width), lambda b: (0, 0)),
            pl.BlockSpec((16, width), lambda b: (0, 0)),
            pl.BlockSpec((8, 128), lambda b: (0, 0)),
            pl.BlockSpec((8, 128), lambda b: (b, 0)),
            pl.BlockSpec((8, 128), lambda b: (b, 0)),
        ],
        compiler_params=params(),
        cost_estimate=pl.CostEstimate(flops=2 * 10**9, bytes_accessed=7 * 10**6, transcendentals=0),
        name="own_margins",
    )(here, total, labels, vectors)


def second_kernel(centres, shifts, second, relay, first, meta, leavers, held_in, two_in, held, two, again, alone, start, goals):
    del held_in, two_in
    half = second.shape[0] - 16
    slots = held.shape[0]
    cap = 2 * slots
    have = count_at(second[half:, :], 5)
    more = count_at(relay[half:, :], 4)
    both = count_at(first[half:, :], 4)
    lane = iota((1, half), 1)
    goal = jnp.where(lane < more, lane + have, -1)
    moved = dot(as_bf(iota((slots, half), 0) == goal), relay[0:half, :]).astype(BF)
    held[0:half, :] = moved[0:half] + second[0:half, :]
    held[half:, :] = moved[half:]
    score = dot_t(centres[...], held[...])
    width = held.shape[1]
    live = iota((1, slots), 1) < have + more
    put_lines(two, 0, jnp.where(live, margins(score, shifts[1:2, 0:1], 2, width), 0.0))

    score = dot_t(centres[...], first[0:half, :])
    value = jnp.where(lane < both, margins(score, shifts[0:1, 0:1], 0, width), 0.0)
    high = value.astype(BF).astype(F32)
    middle = (value - high).astype(BF).astype(F32)
    low = value - high - middle
    value = jnp.concatenate([high, middle, low, jnp.ones((1, half), F32), jnp.zeros((12, half), F32)], axis=0).astype(BF)
    place = jnp.concatenate([meta[k : k + 1, :] for k in range(8)], axis=1)
    goal = jnp.where(lane < both, place[:, :half], -1)
    for k in range(cap // BLK):
        hot = as_bf(iota((BLK, half), 0) + k * BLK == goal)
        got = dot_t(value, hot)
        put_lines(again, k * BLK // 128, got[0:1] + got[1:2] + got[2:3])
        free = (iota((1, BLK), 1) + k * BLK < leavers[0:1, 0:1]) & (got[3:4] < 0.5)
        put_lines(alone, k * BLK // 128, jnp.where(free, 1.0, 0.0))
    lane = iota((8, cap), 1)
    earlier = (lane < both) | (place < BLK * iota((8, cap), 0))
    begin = jnp.sum(jnp.where(earlier, 1.0, 0.0), axis=1, keepdims=True).astype(I32)
    begin = jnp.minimum((begin >> 7) << 7, cap - BLK - 128)
    start[...] = jnp.broadcast_to(begin, start.shape)
    goals[...] = jnp.broadcast_to(jnp.where(iota((1, cap), 1) < both, -1, place), goals.shape)


def second_call(centres, shifts, second, relay, first, meta, leavers, held, two):
    half, width = second.shape
    half -= 16
    cap = 4 * half
    slots = cap // 2
    return pl.pallas_call(
        second_kernel,
        grid=(1,),
        out_shape=[
            jax.ShapeDtypeStruct(held.shape, BF),
            jax.ShapeDtypeStruct(two.shape, F32),
            jax.ShapeDtypeStruct((cap // 128, 128), F32),
            jax.ShapeDtypeStruct((cap // 128, 128), F32),
            jax.ShapeDtypeStruct((8, 128), I32),
            jax.ShapeDtypeStruct((8, cap), I32),
        ],
        in_specs=[spec(pltpu.VMEM)] * 7 + [spec(pl.ANY)] * 2,
        out_specs=[
            pl.BlockSpec((slots, width), lambda b: (held.shape[0] // slots - 1, 0)),
            pl.BlockSpec((slots // 128, 128), lambda b: (held.shape[0] // slots - 1, 0)),
            pl.BlockSpec((cap // 128, 128), lambda b: (0, 0)),
            pl.BlockSpec((cap // 128, 128), lambda b: (0, 0)),
            pl.BlockSpec((8, 128), lambda b: (0, 0)),
            pl.BlockSpec((8, cap), lambda b: (0, 0)),
        ],
        input_output_aliases={7: 0, 8: 1},
        compiler_params=params(),
        cost_estimate=pl.CostEstimate(flops=3 * 10**9, bytes_accessed=6 * 10**6, transcendentals=0),
        name="second_slots",
    )(centres, shifts, second, relay, first, meta, leavers, held, two)


def column_kernel(own, a, b, c, out):
    sums, counts = unpack(own[...])
    for other in (a, b, c):
        s, n = unpack(other[...])
        sums, counts = sums + s, counts + n
    out[0:4, :] = sums
    width = out.shape[1]
    for g in range(4):
        out[4 + g : 5 + g, :] = jnp.broadcast_to(counts[:, 128 * g : 128 * g + 1], (1, width))


def column_call(*pieces):
    width = pieces[0].shape[1]
    return pl.pallas_call(
        column_kernel,
        grid=(1,),
        out_shape=jax.ShapeDtypeStruct((8, width), F32),
        in_specs=[pl.BlockSpec((16, width), functools.partial(lambda last, b: (last, 0), p.shape[0] // 16 - 1)) for p in pieces],
        out_specs=pl.BlockSpec((8, width), lambda b: (0, 0)),
        compiler_params=params(),
        name="column_sums",
    )(*pieces)


def first_kernel(start, centres, shifts, goals, again, alone, first, middle, *refs):
    hands, (held_in, one_in, two_in, held, one, two, x, out, sem, sent) = refs[:HANDS], refs[HANDS:]
    del one_in, two_in, held_in
    part, width = middle.shape
    turns = hands[0].shape[0] // 16
    loads = [
        pltpu.make_async_copy(first.at[pl.ds(0, part)], x.at[pl.ds(0, part)], sem.at[HANDS, 0]),
        pltpu.make_async_copy(middle, x.at[pl.ds(part, part)], sem.at[HANDS, 1]),
    ]
    for h, hand in enumerate(hands):
        for turn in range(turns):
            block = x.at[pl.ds(2 * part + 16 * (h + HANDS * turn), 16)]
            loads.append(pltpu.make_async_copy(hand.at[pl.ds(16 * turn, 16)], block, sem.at[h, turn]))
    for load in loads:
        load.start()
    for load in loads:
        load.wait()
    span = BLK + 128
    base = 8 * part
    slot = iota((BLK, span), 0)
    stores = []
    for k in range(4 * part // BLK):
        begin = pl.multiple_of(start[k, 0], 128)
        hot = as_bf(slot == goals[0:1, pl.ds(begin, span)] - k * BLK)
        rows = dot(hot, x[pl.ds(begin, span), :]).astype(BF)
        lines = pl.ds(k * BLK, BLK)
        out[lines, :] = rows
        stores.append(pltpu.make_async_copy(out.at[lines], held.at[pl.ds(base + k * BLK, BLK)], sent.at[k]))
        stores[-1].start()
        score = dot_t(centres[...], rows)
        m_one = margins(score, shifts[0:1, 0:1], 0, width)
        m_two = margins(score, shifts[1:2, 0:1], 2, width)
        for i in range(BLK // 128):
            line = slice(k * (BLK // 128) + i, k * (BLK // 128) + i + 1)
            lanes = slice(128 * i, 128 * (i + 1))
            one[line, :] = jnp.where(alone[line, :] > 0.5, m_one[:, lanes], again[line, :])
            two[line, :] = jnp.where(alone[line, :] > 0.5, m_two[:, lanes], 0.0)
    for store in stores:
        store.wait()


def first_call(start, centres, shifts, goals, again, alone, first, middle, hands, held, one, two):
    width = held.shape[1]
    cap = goals.shape[1]
    lines = cap // 128
    return pl.pallas_call(
        first_kernel,
        grid=(1,),
        out_shape=[
            jax.ShapeDtypeStruct(held.shape, BF),
            jax.ShapeDtypeStruct(one.shape, F32),
            jax.ShapeDtypeStruct(two.shape, F32),
        ],
        in_specs=[spec(pltpu.SMEM)] + [spec(pltpu.VMEM)] * 5 + [spec(pl.ANY)] * (HANDS + 5),
        out_specs=[
            spec(pl.ANY),
            pl.BlockSpec((lines, 128), lambda k: (2, 0)),
            pl.BlockSpec((lines, 128), lambda k: (2, 0)),
        ],
        scratch_shapes=[
            pltpu.VMEM((cap, width), BF),
            pltpu.VMEM((cap, width), BF),
            pltpu.SemaphoreType.DMA((HANDS + 1, cap // 32 // HANDS)),
            pltpu.SemaphoreType.DMA((cap // BLK,)),
        ],
        input_output_aliases={8 + HANDS: 0, 9 + HANDS: 1, 10 + HANDS: 2},
        compiler_params=params(),
        cost_estimate=pl.CostEstimate(flops=3 * 10**9, bytes_accessed=7 * 10**6, transcendentals=0),
        name="first_slots",
    )(start, centres, shifts, goals, again, alone, first, middle, *hands, held, one, two)


def local(vectors, child_labels):
    ways = lax.axis_size("cube")
    top = ways // 2
    nxt = ways // 4
    me = lax.axis_index("cube")
    here = jnp.stack([(me // top) & 1, (me // nxt) & 1]).astype(I32)
    after = lax.optimization_barrier
    pos, off, every, leavers = plan_call(here, child_labels)
    counts = [leavers] + [swap(leavers, bits) for bits in (nxt, top, top | nxt)]
    first, middle, rest = sort_call(here, child_labels, pos, off, every, vectors)
    first_in = swap(first, top)
    own, *hands = deal_call(rest, *counts)
    hands = [own] + [swap(hand, h + 1) for h, hand in enumerate(hands)]
    after_deal, _ = after((pos, own))
    second, meta = second_send_call(off, after_deal, first, vectors)
    second_in = swap(second, nxt)
    after_send, _ = after((after_deal, meta))
    held = own_call(after_send, vectors)
    limit = rest.shape[0]
    step = limit // 16
    packed, longest, begins = pack_call(step, hands)
    bit = HANDS
    while bit < nxt:
        longest = jnp.maximum(longest, swap(longest, bit))
        bit *= 2

    def cross(size):
        def branch(rows, first_in, meta):
            got = jnp.pad(swap(rows[:size], top), ((0, limit - size), (0, 0))) if size else jnp.zeros_like(rows)
            return got, swap(first_in, nxt), swap(meta, top)

        return branch

    sizes = range(0, limit + 1, step)
    packed, held, first_in = after((packed, held, first_in))
    packed_in, relay, meta_in = lax.switch(longest[0, 0], [cross(size) for size in sizes], packed, first_in, meta)
    middle, packed_in = after((middle, packed_in))
    middle_in = swap(middle, top)
    own, *hands = part_call(begins, packed_in)
    hands = [own] + [swap(hand, h + 1) for h, hand in enumerate(hands)]
    second_in, *hands[4:] = after((second_in, *hands[4:]))
    total = column_call(first, second_in, first_in, relay)
    bit = 1
    while bit < nxt:
        total = total + swap(total, bit)
        bit *= 2
    cents, centres, shifts, one, two = centre_call(here, total, child_labels, vectors)
    held, two, again, alone, start, goals = second_call(
        centres, shifts, second_in, relay, first_in, meta_in, counts[2], held, two
    )
    held, one, two = first_call(
        start, centres, shifts, goals, again, alone, first_in, middle_in, hands, held, one, two
    )
    return held, one.reshape(-1), two.reshape(-1), cents


def solution(mesh):
    return jax.shard_map(
        local,
        mesh=mesh,
        in_specs=(P("cube", None), P(None, "cube")),
        out_specs=(P("cube", None), P("cube"), P("cube"), P()),
        check_vma=False,
    )
```

profile of v0, /device:TPU:0, one launch (start us, length us, event | category | flops | bytes accessed | tf_op | source)
XLA Modules:
  0.0 153.5 jit_solution(4770673173903271190)
XLA Ops:
  1.5 0.9 plan_places.1
  2.4 5.1 %collective-permute-start.52 = (s32[8,128]{1,0:T(8,128)S(1)}, s32[8,128]{1,0:T(8,128)S(1)}, u32[]{:S(2)}, u32[]{:S(2)}) collective-permute-start(s32[8,128]{1,0:T(8,128)S(1)} %get-tuple-element.216.own), channel_id=1, source_target_pairs={{0,24},{1,25},{2,26},{3,27},{4,28},{5,29},{6,30},{7,31},{8,16},{9,... | collective-permute-start | bytes 12296 | tf_op jit(solution)/shard_map/ppermute | solution.py:18
  8.2 9.0 %sort_leavers.1 = (bf16[528,768]{1,0:T(8,128)(2,1)S(1)}, bf16[512,768]{1,0:T(8,128)(2,1)S(1)}, bf16[1024,768]{1,0:T(8,128)(2,1)S(1)}) custom-call(s32[2]{0:T(128)S(1)} %pad_add_fusion.here, s32[2,4096]{1,0:T(2,128)S(1)} %copy-done, s32[128,256]{1,0:T(8,128)S(1)} %get-tuple-element.232.pos_ref.pos, s32[128,128]{1,0:T(8,128)S(1)} %get-tuple-element.212.off_ref.off, ...), custom_call_target="tpu_custom_call" | custom-call | flops 8000000000 | bytes 10000000 | tf_op jit(solution)/shard_map/sort_leavers/pallas_call | solution.py:168
  17.2 2.4 %collective-permute-start.61 = (bf16[528,768]{1,0:T(8,128)(2,1)S(1)}, bf16[528,768]{1,0:T(8,128)(2,1)}, u32[]{:S(2)}, u32[]{:S(2)}) collective-permute-start(bf16[528,768]{1,0:T(8,128)(2,1)S(1)} %get-tuple-element.214.extra.own), channel_id=1, source_target_pairs={{0,16},{1,17},{2,18},{3,19},{4,20},{5,21},{6,22},{7,23},{8,24},{9,... | collective-permute-start | bytes 2433032 | tf_op jit(solution)/shard_map/ppermute | solution.py:18
  19.6 3.1 %deal_rest.1 = (bf16[144,768]{1,0:T(8,128)(2,1)S(1)}, bf16[144,768]{1,0:T(8,128)(2,1)S(1)}, bf16[144,768]{1,0:T(8,128)(2,1)S(1)}, bf16[144,768]{1,0:T(8,128)(2,1...) custom-call(bf16[1024,768]{1,0:T(8,128)(2,1)S(1)} %get-tuple-element, ...), custom_call_target="tpu_custom_call" | custom-call | bytes 3000000 | tf_op jit(solution)/shard_map/deal_rest/pallas_call | solution.py:213
  22.7 6.2 %second_send.1 = (bf16[528,768]{1,0:T(8,128)(2,1)S(1)}, s32[8,256]{1,0:T(8,128)S(1)}) custom-call(s32[128,128]{1,0:T(8,128)S(1)} %get-tuple-element.212.off_ref.off, s32[128,256]{1,0:T(8,128)S(1)} %get-tuple-element.232.pos_ref.pos, bf16[528,768]{1,0:T(8,128)(2,1)S(1)} %get-tuple-element.214.extra.own, bf16[4096,768]{1,0:T(8,128)(2,1)} %x_ref.5), custom_call_target="tpu_custom_call" | custom-call | flops 6000000000 | bytes 8000000 | tf_op jit(solution)/shard_map/second_send/pallas_call | solution.py:340
  28.9 2.0 %collective-permute-start.53 = (bf16[528,768]{1,0:T(8,128)(2,1)S(1)}, bf16[528,768]{1,0:T(8,128)(2,1)S(1)}, u32[]{:S(2)}, u32[]{:S(2)}) collective-permute-start(bf16[528,768]{1,0:T(8,128)(2,1)S(1)} %get-tuple-element.219), channel_id=1, source_target_pairs={{0,8},{1,9},{2,10},{3,11},{4,12},{5,13},{6,14},{7,15},{8,0},{9,1},... | collective-permute-start | bytes 2433032 | tf_op jit(solution)/shard_map/ppermute | solution.py:18
  30.9 1.6 %collective-permute-start.55 = (bf16[144,768]{1,0:T(8,128)(2,1)S(1)}, bf16[144,768]{1,0:T(8,128)(2,1)S(1)}, u32[]{:S(2)}, u32[]{:S(2)}) collective-permute-start(bf16[144,768]{1,0:T(8,128)(2,1)S(1)} %get-tuple-element.221), channel_id=1, source_target_pairs={{0,2},{1,3},{2,0},{3,1},{4,6},{5,7},{6,4},{7,5},{8,10},{9,11},{10,... | collective-permute-start | bytes 663560 | tf_op jit(solution)/shard_map/ppermute | solution.py:18
  32.8 1.6 %collective-permute-start.57 = (bf16[144,768]{1,0:T(8,128)(2,1)S(1)}, bf16[144,768]{1,0:T(8,128)(2,1)S(1)}, u32[]{:S(2)}, u32[]{:S(2)}) collective-permute-start(bf16[144,768]{1,0:T(8,128)(2,1)S(1)} %get-tuple-element.223), channel_id=1, source_target_pairs={{0,4},{1,5},{2,6},{3,7},{4,0},{5,1},{6,2},{7,3},{8,12},{9,13},{10,... | collective-permute-start | bytes 663560 | tf_op jit(solution)/shard_map/ppermute | solution.py:18
  34.3 4.8 %collective-permute-done.55.refs_2_ = bf16[144,768]{1,0:T(8,128)(2,1)S(1)} collective-permute-done((bf16[144,768]{1,0:T(8,128)(2,1)S(1)}, bf16[144,768]{1,0:T(8,128)(2,1)S(1)}, u32[]{:S(2)}, u32[]{:S(2)}) %collective-permute-start.55) | collective-permute-done | bytes 221216 | tf_op jit(solution)/shard_map/ppermute | solution.py:18
  39.7 3.3 %collective-permute-done.56.refs_3_ = bf16[144,768]{1,0:T(8,128)(2,1)S(1)} collective-permute-done((bf16[144,768]{1,0:T(8,128)(2,1)S(1)}, bf16[144,768]{1,0:T(8,128)(2,1)S(1)}, u32[]{:S(2)}, u32[]{:S(2)}) %collective-permute-start.56) | collective-permute-done | bytes 221216 | tf_op jit(solution)/shard_map/ppermute | solution.py:18
  43.1 2.5 %collective-permute-start.59 = (bf16[144,768]{1,0:T(8,128)(2,1)S(1)}, bf16[144,768]{1,0:T(8,128)(2,1)S(1)}, u32[]{:S(2)}, u32[]{:S(2)}) collective-permute-start(bf16[144,768]{1,0:T(8,128)(2,1)S(1)} %get-tuple-element.225), channel_id=1, source_target_pairs={{0,6},{1,7},{2,4},{3,5},{4,2},{5,3},{6,0},{7,1},{8,14},{9,15},{10,... | collective-permute-start | bytes 663560 | tf_op jit(solution)/shard_map/ppermute | solution.py:18
  45.9 6.8 %own_slots.1.held_in = bf16[7168,768]{1,0:T(8,128)(2,1)} custom-call(s32[128,256]{1,0:T(8,128)S(1)} %get-tuple-element.232.pos_ref.pos, bf16[4096,768]{1,0:T(8,128)(2,1)} %x_ref.5), custom_call_target="tpu_custom_call" | custom-call | flops 2000000000 | bytes 13000000 | tf_op jit(solution)/shard_map/own_slots/pallas_call | solution.py:373
  52.8 3.6 %collective-permute-done.60.refs_7_ = bf16[144,768]{1,0:T(8,128)(2,1)S(1)} collective-permute-done((bf16[144,768]{1,0:T(8,128)(2,1)S(1)}, bf16[144,768]{1,0:T(8,128)(2,1)S(1)}, u32[]{:S(2)}, u32[]{:S(2)}) %collective-permute-start.60) | collective-permute-done | bytes 221216 | tf_op jit(solution)/shard_map/ppermute | solution.py:18
  58.0 47.0 %conditional.1 = (bf16[1024,768]{1,0:T(8,128)(2,1)}, bf16[528,768]{1,0:T(8,128)(2,1)}, s32[8,256]{1,0:T(8,128)}) conditional(s32[]{:T(128)} %bitcast.2, (bf16[528,768]{1,0:T(8,128)(2,1)}, s32[8,256]{1,0:T(8,128)S(1)}) %tuple.84, (bf16[1024,768]{1,0:T(8,128)(2,1)S(1)}, bf16[528,768]{1,0:T(8,128)(2,1)}, ...), branch_computations={%region_0.1_spmd, %region_1.2_spmd, %region_2.3_spmd, %region_3.4_... | conditional | bytes 15171730 | solution.py:659
  59.0 2.2 %collective-permute-start.31 = (s32[8,256]{1,0:T(8,128)S(1)}, s32[8,256]{1,0:T(8,128)}, u32[]{:S(2)}, u32[]{:S(2)}) collective-permute-start(s32[8,256]{1,0:T(8,128)S(1)} %get-tuple-element.131), channel_id=1, source_target_pairs={{0,16},{1,17},{2,18},{3,19},{4,20},{5,21},{6,22},{7,23},{8,24},{9,... | collective-permute-start | bytes 24584 | tf_op jit(solution)/shard_map/cond/branch_10_fun/ppermute | solution.py:18
  61.3 42.5 %collective-permute-done.29 = bf16[640,768]{1,0:T(8,128)(2,1)S(1)} collective-permute-done((bf16[640,768]{1,0:T(8,128)(2,1)S(1)}, bf16[640,768]{1,0:T(8,128)(2,1)S(1)}, u32[]{:S(2)}, u32[]{:S(2)}) %collective-permute-start.29) | collective-permute-done | bytes 983072 | tf_op jit(solution)/shard_map/cond/branch_10_fun/ppermute | solution.py:18
  103.7 1.2 pad.54
  105.0 2.1 %part_pack.1 = (bf16[128,768]{1,0:T(8,128)(2,1)S(1)}, bf16[128,768]{1,0:T(8,128)(2,1)S(1)}, bf16[128,768]{1,0:T(8,128)(2,1)S(1)}, bf16[128,768]{1,0:T(8,128)(2,1...) custom-call(s32[8,128]{1,0:T(8,128)S(1)} %get-tuple-element.227.begi, ...), custom_call_target="tpu_custom_call" | custom-call | bytes 3000000 | tf_op jit(solution)/shard_map/part_pack/pallas_call | solution.py:284
  107.1 1.6 %collective-permute-start.62 = (bf16[128,768]{1,0:T(8,128)(2,1)S(1)}, bf16[128,768]{1,0:T(8,128)(2,1)S(1)}, u32[]{:S(2)}, u32[]{:S(2)}) collective-permute-start(bf16[128,768]{1,0:T(8,128)(2,1)S(1)} %get-tuple-element.237), channel_id=1, source_target_pairs={{0,4},{1,5},{2,6},{3,7},{4,0},{5,1},{6,2},{7,3},{8,12},{9,13},{10,... | collective-permute-start | bytes 589832 | tf_op jit(solution)/shard_map/ppermute | solution.py:18
  108.8 2.2 %collective-permute-start.64 = (bf16[128,768]{1,0:T(8,128)(2,1)S(1)}, bf16[128,768]{1,0:T(8,128)(2,1)S(1)}, u32[]{:S(2)}, u32[]{:S(2)}) collective-permute-start(bf16[128,768]{1,0:T(8,128)(2,1)S(1)} %get-tuple-element.239), channel_id=1, source_target_pairs={{0,6},{1,7},{2,4},{3,5},{4,2},{5,3},{6,0},{7,1},{8,14},{9,15},{10,... | collective-permute-start | bytes 589832 | tf_op jit(solution)/shard_map/ppermute | solution.py:18
  111.6 11.8 %collective-permute-done.62.refs_4_ = bf16[128,768]{1,0:T(8,128)(2,1)S(1)} collective-permute-done((bf16[128,768]{1,0:T(8,128)(2,1)S(1)}, bf16[128,768]{1,0:T(8,128)(2,1)S(1)}, u32[]{:S(2)}, u32[]{:S(2)}) %collective-permute-start.62) | collective-permute-done | bytes 196640 | tf_op jit(solution)/shard_map/ppermute | solution.py:18
  123.4 2.3 %collective-permute-done.63.refs_5_ = bf16[128,768]{1,0:T(8,128)(2,1)S(1)} collective-permute-done((bf16[128,768]{1,0:T(8,128)(2,1)S(1)}, bf16[128,768]{1,0:T(8,128)(2,1)S(1)}, u32[]{:S(2)}, u32[]{:S(2)}) %collective-permute-start.63) | collective-permute-done | bytes 196640 | tf_op jit(solution)/shard_map/ppermute | solution.py:18
  125.7 0.9 column_sums.1
  126.6 1.0 collective-permute-start.66
  128.4 1.6 %collective-permute-start.67 = (f32[8,768]{1,0:T(8,128)S(1)}, f32[8,768]{1,0:T(8,128)S(1)}, u32[]{:S(2)}, u32[]{:S(2)}) collective-permute-start(f32[8,768]{1,0:T(8,128)S(1)} %add.41), channel_id=1, source_target_pairs={{0,2},{1,3},{2,0},{3,1},{4,6},{5,7},{6,4},{7,5},{8,10},{9,11},{10,... | collective-permute-start | bytes 73736 | tf_op jit(solution)/shard_map/ppermute | solution.py:18
  130.0 2.3 %collective-permute-done.67 = f32[8,768]{1,0:T(8,128)S(1)} collective-permute-done((f32[8,768]{1,0:T(8,128)S(1)}, f32[8,768]{1,0:T(8,128)S(1)}, u32[]{:S(2)}, u32[]{:S(2)}) %collective-permute-start.67) | collective-permute-done | bytes 24608 | tf_op jit(solution)/shard_map/ppermute | solution.py:18
  132.3 1.6 %collective-permute-start.68 = (f32[8,768]{1,0:T(8,128)S(1)}, f32[8,768]{1,0:T(8,128)S(1)}, u32[]{:S(2)}, u32[]{:S(2)}) collective-permute-start(f32[8,768]{1,0:T(8,128)S(1)} %add.42), channel_id=1, source_target_pairs={{0,4},{1,5},{2,6},{3,7},{4,0},{5,1},{6,2},{7,3},{8,12},{9,13},{10,... | collective-permute-start | bytes 73736 | tf_op jit(solution)/shard_map/ppermute | solution.py:18
  133.9 1.5 collective-permute-start.71
  136.1 5.4 %own_margins.1 = (f32[6,768]{1,0:T(8,128)}, bf16[16,768]{1,0:T(8,128)(2,1)S(1)}, f32[8,128]{1,0:T(8,128)S(1)}, f32[48,128]{1,0:T(8,128)}, f32[56,128]{1,0:T(8,128)}) custom-call(s32[2]{0:T(128)S(1)} %pad_add_fusion.here, f32[8,768]{1,0:T(8,128)S(1)} %add.43.total, s32[2,4096]{1,0:T(2,128)S(1)} %copy-done.1, bf16[4096,768]{1,0:T(8,128)(2,1)} %x_ref.5), custom_call_target="tpu_custom_call" | custom-call | flops 2000000000 | bytes 7000000 | tf_op jit(solution)/shard_map/own_margins/pallas_call | solution.py:427
  141.5 4.2 %second_slots.1 = (bf16[7168,768]{1,0:T(8,128)(2,1)}, f32[56,128]{1,0:T(8,128)}, f32[16,128]{1,0:T(8,128)S(1)}, f32[16,128]{1,0:T(8,128)S(1)}, s32[8,128]{1,0:T(8,128)S(1)}, /*index=5*/s32[8,2048]{1,0:T(8,128)S(1)}) custom-call(bf16[16,768]{1,0:T(8,128)(2,1)S(1)} %get-tuple-element.243.centres, ...), custom_call_target="tpu_custom_call", output_to_operand_aliasing={{0}: (7, {}), {1}: (8, {})} | custom-call | flops 3000000000 | bytes 6000000 | tf_op jit(solution)/shard_map/second_slots/pallas_call | solution.py:501
  145.7 7.6 %first_slots.1 = (bf16[7168,768]{1,0:T(8,128)(2,1)}, f32[48,128]{1,0:T(8,128)}, f32[56,128]{1,0:T(8,128)}) custom-call(s32[8,128]{1,0:T(8,128)S(1)} %get-tuple-element.248.start, bf16[16,768]{1,0:T(8,128)(2,1)S(1)} %get-tuple-element.243.centres, ...), custom_call_target="tpu_custom_call", output_to_operand_aliasing={{0}: (16, {}), {1}: (17, {}), {2}: (18, {})} | custom-call | flops 3000000000 | bytes 7000000 | tf_op jit(solution)/shard_map/first_slots/pallas_call | solution.py:597
  (43 shorter events, 6.8 us)
Async XLA Ops:
  0.7 0.8 copy-start
  2.4 17.2 %collective-permute-start.52 = (s32[8,128]{1,0:T(8,128)S(1)}, s32[8,128]{1,0:T(8,128)S(1)}, u32[]{:S(2)}, u32[]{:S(2)}) collective-permute-start(s32[8,128]{1,0:T(8,128)S(1)} %get-tuple-element.216.own), channel_id=1, source_target_pairs={{0,24},{1,25},{2,26},{3,27},{4,28},{5,29},{6,30},{7,31},{8,16},{9,... | collective-permute-start | bytes 12296 | tf_op jit(solution)/shard_map/ppermute | solution.py:18
  7.5 12.1 %collective-permute-start.51 = (s32[8,128]{1,0:T(8,128)S(1)}, s32[8,128]{1,0:T(8,128)S(1)}, u32[]{:S(2)}, u32[]{:S(2)}) collective-permute-start(s32[8,128]{1,0:T(8,128)S(1)} %get-tuple-element.216.own), channel_id=1, source_target_pairs={{0,16},{1,17},{2,18},{3,19},{4,20},{5,21},{6,22},{7,23},{8,24},{9,... | collective-permute-start | bytes 12296 | tf_op jit(solution)/shard_map/ppermute | solution.py:18
  7.5 12.1 %collective-permute-start.50 = (s32[8,128]{1,0:T(8,128)S(1)}, s32[8,128]{1,0:T(8,128)S(1)}, u32[]{:S(2)}, u32[]{:S(2)}) collective-permute-start(s32[8,128]{1,0:T(8,128)S(1)} %get-tuple-element.216.own), channel_id=1, source_target_pairs={{0,8},{1,9},{2,10},{3,11},{4,12},{5,13},{6,14},{7,15},{8,0},{9,1},... | collective-permute-start | bytes 12296 | tf_op jit(solution)/shard_map/ppermute | solution.py:18
  17.2 40.8 %collective-permute-start.61 = (bf16[528,768]{1,0:T(8,128)(2,1)S(1)}, bf16[528,768]{1,0:T(8,128)(2,1)}, u32[]{:S(2)}, u32[]{:S(2)}) collective-permute-start(bf16[528,768]{1,0:T(8,128)(2,1)S(1)} %get-tuple-element.214.extra.own), channel_id=1, source_target_pairs={{0,16},{1,17},{2,18},{3,19},{4,20},{5,21},{6,22},{7,23},{8,24},{9,... | collective-permute-start | bytes 2433032 | tf_op jit(solution)/shard_map/ppermute | solution.py:18
  28.9 82.1 %collective-permute-start.53 = (bf16[528,768]{1,0:T(8,128)(2,1)S(1)}, bf16[528,768]{1,0:T(8,128)(2,1)S(1)}, u32[]{:S(2)}, u32[]{:S(2)}) collective-permute-start(bf16[528,768]{1,0:T(8,128)(2,1)S(1)} %get-tuple-element.219), channel_id=1, source_target_pairs={{0,8},{1,9},{2,10},{3,11},{4,12},{5,13},{6,14},{7,15},{8,0},{9,1},... | collective-permute-start | bytes 2433032 | tf_op jit(solution)/shard_map/ppermute | solution.py:18
  30.9 1.9 %collective-permute-start.54 = (bf16[144,768]{1,0:T(8,128)(2,1)S(1)}, bf16[144,768]{1,0:T(8,128)(2,1)S(1)}, u32[]{:S(2)}, u32[]{:S(2)}) collective-permute-start(bf16[144,768]{1,0:T(8,128)(2,1)S(1)} %get-tuple-element.220), channel_id=1, source_target_pairs={{0,1},{1,0},{2,3},{3,2},{4,5},{5,4},{6,7},{7,6},{8,9},{9,8},{10,11... | collective-permute-start | bytes 663560 | tf_op jit(solution)/shard_map/ppermute | solution.py:18
  30.9 8.2 %collective-permute-start.55 = (bf16[144,768]{1,0:T(8,128)(2,1)S(1)}, bf16[144,768]{1,0:T(8,128)(2,1)S(1)}, u32[]{:S(2)}, u32[]{:S(2)}) collective-permute-start(bf16[144,768]{1,0:T(8,128)(2,1)S(1)} %get-tuple-element.221), channel_id=1, source_target_pairs={{0,2},{1,3},{2,0},{3,1},{4,6},{5,7},{6,4},{7,5},{8,10},{9,11},{10,... | collective-permute-start | bytes 663560 | tf_op jit(solution)/shard_map/ppermute | solution.py:18
  32.5 10.6 %collective-permute-start.56 = (bf16[144,768]{1,0:T(8,128)(2,1)S(1)}, bf16[144,768]{1,0:T(8,128)(2,1)S(1)}, u32[]{:S(2)}, u32[]{:S(2)}) collective-permute-start(bf16[144,768]{1,0:T(8,128)(2,1)S(1)} %get-tuple-element.222), channel_id=1, source_target_pairs={{0,3},{1,2},{2,1},{3,0},{4,7},{5,6},{6,5},{7,4},{8,11},{9,10},{10,... | collective-permute-start | bytes 663560 | tf_op jit(solution)/shard_map/ppermute | solution.py:18
  32.8 12.8 %collective-permute-start.57 = (bf16[144,768]{1,0:T(8,128)(2,1)S(1)}, bf16[144,768]{1,0:T(8,128)(2,1)S(1)}, u32[]{:S(2)}, u32[]{:S(2)}) collective-permute-start(bf16[144,768]{1,0:T(8,128)(2,1)S(1)} %get-tuple-element.223), channel_id=1, source_target_pairs={{0,4},{1,5},{2,6},{3,7},{4,0},{5,1},{6,2},{7,3},{8,12},{9,13},{10,... | collective-permute-start | bytes 663560 | tf_op jit(solution)/shard_map/ppermute | solution.py:18
  39.1 13.7 %collective-permute-start.58 = (bf16[144,768]{1,0:T(8,128)(2,1)S(1)}, bf16[144,768]{1,0:T(8,128)(2,1)S(1)}, u32[]{:S(2)}, u32[]{:S(2)}) collective-permute-start(bf16[144,768]{1,0:T(8,128)(2,1)S(1)} %get-tuple-element.224), channel_id=1, source_target_pairs={{0,5},{1,4},{2,7},{3,6},{4,1},{5,0},{6,3},{7,2},{8,13},{9,12},{10,... | collective-permute-start | bytes 663560 | tf_op jit(solution)/shard_map/ppermute | solution.py:18
  43.1 9.7 %collective-permute-start.59 = (bf16[144,768]{1,0:T(8,128)(2,1)S(1)}, bf16[144,768]{1,0:T(8,128)(2,1)S(1)}, u32[]{:S(2)}, u32[]{:S(2)}) collective-permute-start(bf16[144,768]{1,0:T(8,128)(2,1)S(1)} %get-tuple-element.225), channel_id=1, source_target_pairs={{0,6},{1,7},{2,4},{3,5},{4,2},{5,3},{6,0},{7,1},{8,14},{9,15},{10,... | collective-permute-start | bytes 663560 | tf_op jit(solution)/shard_map/ppermute | solution.py:18
  45.6 10.8 %collective-permute-start.60 = (bf16[144,768]{1,0:T(8,128)(2,1)S(1)}, bf16[144,768]{1,0:T(8,128)(2,1)S(1)}, u32[]{:S(2)}, u32[]{:S(2)}) collective-permute-start(bf16[144,768]{1,0:T(8,128)(2,1)S(1)} %get-tuple-element.226), channel_id=1, source_target_pairs={{0,7},{1,6},{2,5},{3,4},{4,3},{5,2},{6,1},{7,0},{8,15},{9,14},{10,... | collective-permute-start | bytes 663560 | tf_op jit(solution)/shard_map/ppermute | solution.py:18
  58.3 45.5 %collective-permute-start.29 = (bf16[640,768]{1,0:T(8,128)(2,1)S(1)}, bf16[640,768]{1,0:T(8,128)(2,1)S(1)}, u32[]{:S(2)}, u32[]{:S(2)}) collective-permute-start(bf16[640,768]{1,0:T(8,128)(2,1)S(1)} %slice.41), channel_id=1, source_target_pairs={{0,16},{1,17},{2,18},{3,19},{4,20},{5,21},{6,22},{7,23},{8,24},{9,... | collective-permute-start | bytes 2949128 | tf_op jit(solution)/shard_map/cond/branch_10_fun/ppermute | solution.py:18
  58.3 46.6 %collective-permute-start.30 = (bf16[528,768]{1,0:T(8,128)(2,1)}, bf16[528,768]{1,0:T(8,128)(2,1)}, u32[]{:S(2)}, u32[]{:S(2)}) collective-permute-start(bf16[528,768]{1,0:T(8,128)(2,1)} %get-tuple-element.130), channel_id=1, source_target_pairs={{0,8},{1,9},{2,10},{3,11},{4,12},{5,13},{6,14},{7,15},{8,0},{9,1},... | collective-permute-start | bytes 2433032 | tf_op jit(solution)/shard_map/cond/branch_10_fun/ppermute | solution.py:18
  59.0 45.9 %collective-permute-start.31 = (s32[8,256]{1,0:T(8,128)S(1)}, s32[8,256]{1,0:T(8,128)}, u32[]{:S(2)}, u32[]{:S(2)}) collective-permute-start(s32[8,256]{1,0:T(8,128)S(1)} %get-tuple-element.131), channel_id=1, source_target_pairs={{0,16},{1,17},{2,18},{3,19},{4,20},{5,21},{6,22},{7,23},{8,24},{9,... | collective-permute-start | bytes 24584 | tf_op jit(solution)/shard_map/cond/branch_10_fun/ppermute | solution.py:18
  105.0 40.8 %collective-permute-start.69 = (bf16[512,768]{1,0:T(8,128)(2,1)S(1)}, bf16[512,768]{1,0:T(8,128)(2,1)S(1)}, u32[]{:S(2)}, u32[]{:S(2)}) collective-permute-start(bf16[512,768]{1,0:T(8,128)(2,1)S(1)} %get-tuple-element.252), channel_id=1, source_target_pairs={{0,16},{1,17},{2,18},{3,19},{4,20},{5,21},{6,22},{7,23},{8,24},{9,... | collective-permute-start | bytes 2359304 | tf_op jit(solution)/shard_map/ppermute | solution.py:18
  107.1 16.3 %collective-permute-start.62 = (bf16[128,768]{1,0:T(8,128)(2,1)S(1)}, bf16[128,768]{1,0:T(8,128)(2,1)S(1)}, u32[]{:S(2)}, u32[]{:S(2)}) collective-permute-start(bf16[128,768]{1,0:T(8,128)(2,1)S(1)} %get-tuple-element.237), channel_id=1, source_target_pairs={{0,4},{1,5},{2,6},{3,7},{4,0},{5,1},{6,2},{7,3},{8,12},{9,13},{10,... | collective-permute-start | bytes 589832 | tf_op jit(solution)/shard_map/ppermute | solution.py:18
  108.8 16.9 %collective-permute-start.63 = (bf16[128,768]{1,0:T(8,128)(2,1)S(1)}, bf16[128,768]{1,0:T(8,128)(2,1)S(1)}, u32[]{:S(2)}, u32[]{:S(2)}) collective-permute-start(bf16[128,768]{1,0:T(8,128)(2,1)S(1)} %get-tuple-element.238), channel_id=1, source_target_pairs={{0,5},{1,4},{2,7},{3,6},{4,1},{5,0},{6,3},{7,2},{8,13},{9,12},{10,... | collective-permute-start | bytes 589832 | tf_op jit(solution)/shard_map/ppermute | solution.py:18
  108.8 16.9 %collective-permute-start.64 = (bf16[128,768]{1,0:T(8,128)(2,1)S(1)}, bf16[128,768]{1,0:T(8,128)(2,1)S(1)}, u32[]{:S(2)}, u32[]{:S(2)}) collective-permute-start(bf16[128,768]{1,0:T(8,128)(2,1)S(1)} %get-tuple-element.239), channel_id=1, source_target_pairs={{0,6},{1,7},{2,4},{3,5},{4,2},{5,3},{6,0},{7,1},{8,14},{9,15},{10,... | collective-permute-start | bytes 589832 | tf_op jit(solution)/shard_map/ppermute | solution.py:18
  111.0 14.7 %collective-permute-start.65 = (bf16[128,768]{1,0:T(8,128)(2,1)S(1)}, bf16[128,768]{1,0:T(8,128)(2,1)S(1)}, u32[]{:S(2)}, u32[]{:S(2)}) collective-permute-start(bf16[128,768]{1,0:T(8,128)(2,1)S(1)} %get-tuple-element.240), channel_id=1, source_target_pairs={{0,7},{1,6},{2,5},{3,4},{4,3},{5,2},{6,1},{7,0},{8,15},{9,14},{10,... | collective-permute-start | bytes 589832 | tf_op jit(solution)/shard_map/ppermute | solution.py:18
  125.7 10.4 %copy-start.1 = (s32[2,4096]{1,0:T(2,128)S(1)}, s32[2,4096]{1,0:T(2,128)}, u32[]{:S(2)}) copy-start(s32[2,4096]{1,0:T(2,128)} %labels.5) | copy-start | bytes 98308
  126.6 1.9 %collective-permute-start.66 = (f32[8,768]{1,0:T(8,128)S(1)}, f32[8,768]{1,0:T(8,128)S(1)}, u32[]{:S(2)}, u32[]{:S(2)}) collective-permute-start(f32[8,768]{1,0:T(8,128)S(1)} %column_sums.1), channel_id=1, source_target_pairs={{0,1},{1,0},{2,3},{3,2},{4,5},{5,4},{6,7},{7,6},{8,9},{9,8},{10,11... | collective-permute-start | bytes 73736 | tf_op jit(solution)/shard_map/ppermute | solution.py:18
  128.4 3.8 %collective-permute-start.67 = (f32[8,768]{1,0:T(8,128)S(1)}, f32[8,768]{1,0:T(8,128)S(1)}, u32[]{:S(2)}, u32[]{:S(2)}) collective-permute-start(f32[8,768]{1,0:T(8,128)S(1)} %add.41), channel_id=1, source_target_pairs={{0,2},{1,3},{2,0},{3,1},{4,6},{5,7},{6,4},{7,5},{8,10},{9,11},{10,... | collective-permute-start | bytes 73736 | tf_op jit(solution)/shard_map/ppermute | solution.py:18
  132.3 3.8 %collective-permute-start.68 = (f32[8,768]{1,0:T(8,128)S(1)}, f32[8,768]{1,0:T(8,128)S(1)}, u32[]{:S(2)}, u32[]{:S(2)}) collective-permute-start(f32[8,768]{1,0:T(8,128)S(1)} %add.42), channel_id=1, source_target_pairs={{0,4},{1,5},{2,6},{3,7},{4,0},{5,1},{6,2},{7,3},{8,12},{9,13},{10,... | collective-permute-start | bytes 73736 | tf_op jit(solution)/shard_map/ppermute | solution.py:18
  133.8 11.9 %collective-permute-start.70 = (bf16[128,768]{1,0:T(8,128)(2,1)S(1)}, bf16[128,768]{1,0:T(8,128)(2,1)S(1)}, u32[]{:S(2)}, u32[]{:S(2)}) collective-permute-start(bf16[128,768]{1,0:T(8,128)(2,1)S(1)} %get-tuple-element.254), channel_id=1, source_target_pairs={{0,1},{1,0},{2,3},{3,2},{4,5},{5,4},{6,7},{7,6},{8,9},{9,8},{10,11... | collective-permute-start | bytes 589832 | tf_op jit(solution)/shard_map/ppermute | solution.py:18
  133.9 11.9 %collective-permute-start.71 = (bf16[128,768]{1,0:T(8,128)(2,1)S(1)}, bf16[128,768]{1,0:T(8,128)(2,1)S(1)}, u32[]{:S(2)}, u32[]{:S(2)}) collective-permute-start(bf16[128,768]{1,0:T(8,128)(2,1)S(1)} %get-tuple-element.255), channel_id=1, source_target_pairs={{0,2},{1,3},{2,0},{3,1},{4,6},{5,7},{6,4},{7,5},{8,10},{9,11},{10,... | collective-permute-start | bytes 589832 | tf_op jit(solution)/shard_map/ppermute | solution.py:18
  135.3 10.4 %collective-permute-start.72 = (bf16[128,768]{1,0:T(8,128)(2,1)S(1)}, bf16[128,768]{1,0:T(8,128)(2,1)S(1)}, u32[]{:S(2)}, u32[]{:S(2)}) collective-permute-start(bf16[128,768]{1,0:T(8,128)(2,1)S(1)} %get-tuple-element.256), channel_id=1, source_target_pairs={{0,3},{1,2},{2,1},{3,0},{4,7},{5,6},{6,5},{7,4},{8,11},{9,10},{10,... | collective-permute-start | bytes 589832 | tf_op jit(solution)/shard_map/ppermute | solution.py:18
where the time goes:
time: 154 us
  waiting for transfers between devices  71.8 us (47%)
  Pallas kernels  46.6 us (30%)
  starting transfers between devices  30.6 us (20%)
  local copies, waits for them, and re-layouts  2.58 us (2%)
  between operations  1.58 us (1%)
    ppermute x26, waiting for transfers between devices, swap(): lax.ppermute(x, 'cube', [(i, i ^ bits) for i in range(lax.axis_size('cube...  71.8 us
    ppermute x26, starting transfers between devices, swap(): lax.ppermute(x, 'cube', [(i, i ^ bits) for i in range(lax.axis_size('cube...  30.6 us
    pallas_call x1, Pallas kernels, sort_call(): pl.pallas_call(sort_kernel, out_shape=[jax.ShapeDtypeStruct((part + 16, w...  9.03 us
    pallas_call x1, Pallas kernels, first_call(): pl.pallas_call(first_kernel, grid=(1,), out_shape=[jax.ShapeDtypeStruct(h...  7.62 us
    pallas_call x1, Pallas kernels, own_call(): pl.pallas_call(own_kernel, grid=(rows // 1024,), out_shape=jax.ShapeDtype...  6.84 us
    pallas_call x1, Pallas kernels, second_send_call(): pl.pallas_call(second_send_kernel, grid=(rows // 1024,), out_shape=[jax.S...  6.17 us
    pallas_call x1, Pallas kernels, centre_call(): pl.pallas_call(centre_kernel, grid=(rows // 1024,), out_shape=[jax.ShapeD...  5.43 us
    pallas_call x1, Pallas kernels, second_call(): pl.pallas_call(second_kernel, grid=(1,), out_shape=[jax.ShapeDtypeStruct(...  4.17 us
  transfers between devices with their start and end apart: 26, of which 9 were waited for; matrix products, arithmetic and copies ran while one was open for 1% of the time, Pallas kernels for 25%

commit v1 on v0

--- a/solution.py
+++ b/solution.py
@@ -11,6 +11,7 @@
 I32 = jnp.int32
 BLK = 256
 HANDS = 8
+WIDE = BLK // 2 + 16
 VMEM_BYTES = 48 * 1024 * 1024
 
 
@@ -84,7 +85,7 @@
     earlier = as_bf((same & (c < r)) | (((r & 7) == 1) & ((c & 7) == 0)))
     off = dot(earlier, total)
     pos[...] = jnp.where(mask, (before + off).astype(I32) - 1, -1)
-    off_ref[...] = off[:, :128].astype(I32)
+    off_ref[...] = (off + jnp.where(iota((tall, BLK), 1) < 64, 0.0, total.astype(F32)))[:, :128].astype(I32)
     r8, c8 = iota((8, tall), 0), iota((8, tall), 1)
     count = dot(as_bf(r8 == (c8 & 7)), total)[:, :128].astype(I32)
     every[...] = count
@@ -110,7 +111,7 @@
     )(here, labels)
 
 
-def sort_kernel(here, labels, pos_ref, off_ref, every, x_hbm, first, middle, rest, x, buf, tail, sem_in, sem_out):
+def sort_kernel(here, labels, pos_ref, off_ref, every, x_hbm, first, middle, rest, x, buf, tail, sums, sem_in, sem_out):
     rows = labels.shape[1]
     blocks = rows // BLK
     cap = rows // 2
@@ -123,32 +124,44 @@
         load.start()
     buf[...] = jnp.zeros_like(buf)
     group = 2 * labels[0:1, :] + labels[1:2, :]
-    wide = BLK + 16
-    slot = iota((wide, BLK), 0)
-    sums = jnp.zeros((4, x.shape[1]), F32)
+    slot = iota((WIDE, BLK), 0)
+    more_slot = iota((BLK + 16 - WIDE, BLK), 0) + WIDE
+    sums[...] = jnp.zeros_like(sums)
     for b in range(blocks):
         if b % (step // BLK) == 0:
             loads[b // (step // BLK)].wait()
-        hot = []
+        vectors = x.at[pl.ds(b * BLK, BLK)]
+        hot = [as_bf((iota((16, BLK), 0) & 3) == group[:, b * BLK : (b + 1) * BLK])]
         bases = []
+        ends = []
+        places = []
         for kind in (0, 1):
-            base = off_ref[8 * b + kind : 8 * b + kind + 1, 0:1]
-            base = jnp.minimum((base[0, 0] // 16) * 16, cap)
-            place = pos_ref[8 * b + kind : 8 * b + kind + 1, :]
-            hot.append(as_bf(slot == place - base))
-            bases.append(pl.multiple_of(base, 16))
-        hot.append(as_bf((iota((16, BLK), 0) & 3) == group[:, b * BLK : (b + 1) * BLK]))
-        got = dot(jnp.concatenate(hot, axis=0), x[b * BLK : (b + 1) * BLK, :])
+            line = slice(8 * b + kind, 8 * b + kind + 1)
+            base = pl.multiple_of(jnp.minimum((off_ref[line, 0:1][0, 0] // 16) * 16, cap), 16)
+            bases.append(base)
+            ends.append(off_ref[line, 64:65][0, 0])
+            places.append(pos_ref[line, :] - base)
+            hot.append(as_bf(slot == places[kind]))
+        got = dot(jnp.concatenate(hot, axis=0), vectors[...])
+        sums[...] += got[0:8]
+        got = got[16:].astype(BF)
+        buf[pl.ds(bases[0], WIDE), :] += got[:WIDE]
+        buf[pl.ds(bases[1], 16), :] += got[WIDE : WIDE + 16]
+        buf[pl.ds(bases[1] + 16, WIDE - 16), :] = got[WIDE + 16 :]
         for kind in (0, 1):
-            buf[pl.ds(bases[kind], wide), :] += got[kind * wide : (kind + 1) * wide].astype(BF)
-        sums += got[2 * wide : 2 * wide + 4]
+
+            @pl.when(ends[kind] - bases[kind] > WIDE)
+            def _():
+                more = dot(as_bf(more_slot == places[kind]), vectors[...]).astype(BF)
+                buf[pl.ds(bases[kind] + WIDE, BLK + 16 - WIDE), :] += more
+
     one, two = here[0], here[1]
     kinds = [every[k : k + 1] for k in range(4)]
     counts = []
     for g in range(4):
         away, miss = jnp.int32(g >> 1) != one, jnp.int32(g & 1) != two
         counts.append(jnp.where(away, jnp.where(miss, kinds[0], kinds[1]), jnp.where(miss, kinds[2], kinds[3])))
-    tail[...] = pack(sums, counts + [kinds[0], kinds[2]], x.shape[1])
+    tail[...] = pack(sums[0:4, :], counts + [kinds[0], kinds[2]], x.shape[1])
     part = cap // 4
     stores = [
         pltpu.make_async_copy(buf.at[pl.ds(0, part)], first.at[pl.ds(0, part)], sem_out.at[0]),
@@ -178,6 +191,7 @@
             pltpu.VMEM((rows, width), BF),
             pltpu.VMEM((rows // 2 + BLK + 16, width), BF),
             pltpu.VMEM((16, width), BF),
+            pltpu.VMEM((8, width), F32),
             pltpu.SemaphoreType.DMA((4,)),
             pltpu.SemaphoreType.DMA((4,)),
         ],
@@ -394,7 +408,7 @@
         ref[start + k : start + k + 1, :] = values[:, 128 * k : 128 * (k + 1)]
 
 
-def centre_kernel(here, total, labels, x_ref, cents, centres, shifts, one, two):
+def centre_kernel(here, total, labels, x_ref, cents, centres, turned, shifts, one, two):
     width = x_ref.shape[1]
 
     @pl.when(pl.program_id(0) == 0)
@@ -409,12 +423,14 @@
         top = here[0] == 1
         left = jnp.where(top, groups[2:3], groups[0:1])
         right = jnp.where(top, groups[3:4], groups[1:2])
-        centres[...] = jnp.concatenate([low, high, left, right, jnp.zeros((12, width), F32)], axis=0).astype(BF)
+        rows = jnp.concatenate([low, high, left, right, jnp.zeros((124, width), F32)], axis=0)
+        centres[...] = rows[0:16].astype(BF)
+        turned[...] = rows.T.astype(BF)
         for k, (a, b) in enumerate(((low, high), (left, right))):
             shift = 0.5 * (jnp.sum(b * b, axis=1, keepdims=True) - jnp.sum(a * a, axis=1, keepdims=True))
             shifts[k : k + 1, :] = jnp.broadcast_to(shift, (1, 128))
 
-    score = dot_t(centres[...], x_ref[...])
+    score = dot(x_ref[...], turned[...]).T
     stay = labels[0:1, :] == here[0]
     keep = stay & (labels[1:2, :] == here[1])
     put_lines(one, 0, jnp.where(stay, margins(score, shifts[0:1, 0:1], 0, width), 0.0))
@@ -430,6 +446,7 @@
         out_shape=[
             jax.ShapeDtypeStruct((6, width), F32),
             jax.ShapeDtypeStruct((16, width), BF),
+            jax.ShapeDtypeStruct((width, 128), BF),
             jax.ShapeDtypeStruct((8, 128), F32),
             jax.ShapeDtypeStruct(((rows + cap) // 128, 128), F32),
             jax.ShapeDtypeStruct(((rows + cap + cap // 2) // 128, 128), F32),
@@ -443,6 +460,7 @@
         out_specs=[
             pl.BlockSpec((6, width), lambda b: (0, 0)),
             pl.BlockSpec((16, width), lambda b: (0, 0)),
+            pl.BlockSpec((width, 128), lambda b: (0, 0)),
             pl.BlockSpec((8, 128), lambda b: (0, 0)),
             pl.BlockSpec((8, 128), lambda b: (b, 0)),
             pl.BlockSpec((8, 128), lambda b: (b, 0)),
@@ -549,7 +567,7 @@
     )(*pieces)
 
 
-def first_kernel(start, centres, shifts, goals, again, alone, first, middle, *refs):
+def first_kernel(start, turned, shifts, goals, again, alone, first, middle, *refs):
     hands, (held_in, one_in, two_in, held, one, two, x, out, sem, sent) = refs[:HANDS], refs[HANDS:]
     del one_in, two_in, held_in
     part, width = middle.shape
@@ -578,7 +596,7 @@
         out[lines, :] = rows
         stores.append(pltpu.make_async_copy(out.at[lines], held.at[pl.ds(base + k * BLK, BLK)], sent.at[k]))
         stores[-1].start()
-        score = dot_t(centres[...], rows)
+        score = dot(rows, turned[...]).T
         m_one = margins(score, shifts[0:1, 0:1], 0, width)
         m_two = margins(score, shifts[1:2, 0:1], 2, width)
         for i in range(BLK // 128):
@@ -590,7 +608,7 @@
         store.wait()
 
 
-def first_call(start, centres, shifts, goals, again, alone, first, middle, hands, held, one, two):
+def first_call(start, turned, shifts, goals, again, alone, first, middle, hands, held, one, two):
     width = held.shape[1]
     cap = goals.shape[1]
     lines = cap // 128
@@ -618,7 +636,7 @@
         compiler_params=params(),
         cost_estimate=pl.CostEstimate(flops=3 * 10**9, bytes_accessed=7 * 10**6, transcendentals=0),
         name="first_slots",
-    )(start, centres, shifts, goals, again, alone, first, middle, *hands, held, one, two)
+    )(start, turned, shifts, goals, again, alone, first, middle, *hands, held, one, two)
 
 
 def local(vectors, child_labels):
@@ -661,18 +679,18 @@
     middle_in = swap(middle, top)
     own, *hands = part_call(begins, packed_in)
     hands = [own] + [swap(hand, h + 1) for h, hand in enumerate(hands)]
-    second_in, *hands[4:] = after((second_in, *hands[4:]))
+    second_in, hands[1] = after((second_in, hands[1]))
     total = column_call(first, second_in, first_in, relay)
     bit = 1
     while bit < nxt:
         total = total + swap(total, bit)
         bit *= 2
-    cents, centres, shifts, one, two = centre_call(here, total, child_labels, vectors)
+    cents, centres, turned, shifts, one, two = centre_call(here, total, child_labels, vectors)
     held, two, again, alone, start, goals = second_call(
         centres, shifts, second_in, relay, first_in, meta_in, counts[2], held, two
     )
     held, one, two = first_call(
-        start, centres, shifts, goals, again, alone, first_in, middle_in, hands, held, one, two
+        start, turned, shifts, goals, again, alone, first_in, middle_in, hands, held, one, two
     )
     return held, one.reshape(-1), two.reshape(-1), cents
 

time: 154 us -> 151 us (0.981)
  starting transfers between devices: 30.6 us -> 28.6 us
    ppermute x26, starting transfers between devices: 30.6 us -> 28.6 us  [swap(): lax.ppermute(x, 'cube', [(i, i ^ bits) for i in range(lax.axis_size('cube...]
  transfers between devices with their start and end apart: 26 -> 26, of which waited for: 9 -> 11; matrix products, arithmetic and copies ran while one was open for 1% -> 1% of each run, Pallas kernels for 25% -> 25%
where the time goes in v1:
time: 151 us
  waiting for transfers between devices  71.4 us (47%)
  Pallas kernels  46.4 us (31%)
  starting transfers between devices  28.6 us (19%)
  local copies, waits for them, and re-layouts  2.58 us (2%)
  between operations  1.61 us (1%)
    ppermute x26, waiting for transfers between devices, swap(): lax.ppermute(x, 'cube', [(i, i ^ bits) for i in range(lax.axis_size('cube...  71.4 us
    ppermute x26, starting transfers between devices, swap(): lax.ppermute(x, 'cube', [(i, i ^ bits) for i in range(lax.axis_size('cube...  28.6 us
    pallas_call x1, Pallas kernels, sort_call(): pl.pallas_call(sort_kernel, out_shape=[jax.ShapeDtypeStruct((part + 16, w...  8.39 us
    pallas_call x1, Pallas kernels, first_call(): pl.pallas_call(first_kernel, grid=(1,), out_shape=[jax.ShapeDtypeStruct(h...  7.66 us
    pallas_call x1, Pallas kernels, own_call(): pl.pallas_call(own_kernel, grid=(rows // 1024,), out_shape=jax.ShapeDtype...  6.84 us
    pallas_call x1, Pallas kernels, second_send_call(): pl.pallas_call(second_send_kernel, grid=(rows // 1024,), out_shape=[jax.S...  6.2 us
    pallas_call x1, Pallas kernels, centre_call(): pl.pallas_call(centre_kernel, grid=(rows // 1024,), out_shape=[jax.ShapeD...  5.79 us
    pallas_call x1, Pallas kernels, second_call(): pl.pallas_call(second_kernel, grid=(1,), out_shape=[jax.ShapeDtypeStruct(...  4.17 us
  transfers between devices with their start and end apart: 26, of which 11 were waited for; matrix products, arithmetic and copies ran while one was open for 1% of the time, Pallas kernels for 25%

profile of v1, /device:TPU:0, one launch (start us, length us, event | category | flops | bytes accessed | tf_op | source)
XLA Modules:
  0.0 150.9 jit_solution(3627534265047198339)
XLA Ops:
  2.4 5.1 %collective-permute-start.52 = (s32[8,128]{1,0:T(8,128)S(1)}, s32[8,128]{1,0:T(8,128)S(1)}, u32[]{:S(2)}, u32[]{:S(2)}) collective-permute-start(s32[8,128]{1,0:T(8,128)S(1)} %get-tuple-element.214.own), channel_id=1, source_target_pairs={{0,24},{1,25},{2,26},{3,27},{4,28},{5,29},{6,30},{7,31},{8,16},{9,... | collective-permute-start | bytes 12296 | tf_op jit(solution)/shard_map/ppermute | solution.py:19
  8.2 8.4 %sort_leavers.1 = (bf16[528,768]{1,0:T(8,128)(2,1)S(1)}, bf16[512,768]{1,0:T(8,128)(2,1)S(1)}, bf16[1024,768]{1,0:T(8,128)(2,1)S(1)}) custom-call(s32[2]{0:T(128)S(1)} %pad_add_fusion.here, s32[2,4096]{1,0:T(2,128)S(1)} %copy-done, s32[128,256]{1,0:T(8,128)S(1)} %get-tuple-element.230.pos_ref.pos, s32[128,128]{1,0:T(8,128)S(1)} %get-tuple-element.210.off_ref.off, ...), custom_call_target="tpu_custom_call" | custom-call | flops 8000000000 | bytes 10000000 | tf_op jit(solution)/shard_map/sort_leavers/pallas_call | solution.py:181
  16.6 2.4 %collective-permute-start.61 = (bf16[528,768]{1,0:T(8,128)(2,1)S(1)}, bf16[528,768]{1,0:T(8,128)(2,1)}, u32[]{:S(2)}, u32[]{:S(2)}) collective-permute-start(bf16[528,768]{1,0:T(8,128)(2,1)S(1)} %get-tuple-element.212.extra.own), channel_id=1, source_target_pairs={{0,16},{1,17},{2,18},{3,19},{4,20},{5,21},{6,22},{7,23},{8,24},{9,... | collective-permute-start | bytes 2433032 | tf_op jit(solution)/shard_map/ppermute | solution.py:19
  18.9 3.1 %deal_rest.1 = (bf16[144,768]{1,0:T(8,128)(2,1)S(1)}, bf16[144,768]{1,0:T(8,128)(2,1)S(1)}, bf16[144,768]{1,0:T(8,128)(2,1)S(1)}, bf16[144,768]{1,0:T(8,128)(2,1...) custom-call(bf16[1024,768]{1,0:T(8,128)(2,1)S(1)} %get-tuple-element, ...), custom_call_target="tpu_custom_call" | custom-call | bytes 3000000 | tf_op jit(solution)/shard_map/deal_rest/pallas_call | solution.py:227
  22.1 6.2 %second_send.1 = (bf16[528,768]{1,0:T(8,128)(2,1)S(1)}, s32[8,256]{1,0:T(8,128)S(1)}) custom-call(s32[128,128]{1,0:T(8,128)S(1)} %get-tuple-element.210.off_ref.off, s32[128,256]{1,0:T(8,128)S(1)} %get-tuple-element.230.pos_ref.pos, bf16[528,768]{1,0:T(8,128)(2,1)S(1)} %get-tuple-element.212.extra.own, bf16[4096,768]{1,0:T(8,128)(2,1)} %x_ref.5), custom_call_target="tpu_custom_call" | custom-call | flops 6000000000 | bytes 8000000 | tf_op jit(solution)/shard_map/second_send/pallas_call | solution.py:354
  28.3 2.1 %collective-permute-start.53 = (bf16[528,768]{1,0:T(8,128)(2,1)S(1)}, bf16[528,768]{1,0:T(8,128)(2,1)S(1)}, u32[]{:S(2)}, u32[]{:S(2)}) collective-permute-start(bf16[528,768]{1,0:T(8,128)(2,1)S(1)} %get-tuple-element.217), channel_id=1, source_target_pairs={{0,8},{1,9},{2,10},{3,11},{4,12},{5,13},{6,14},{7,15},{8,0},{9,1},... | collective-permute-start | bytes 2433032 | tf_op jit(solution)/shard_map/ppermute | solution.py:19
  30.4 1.5 collective-permute-start.55
  31.9 1.5 collective-permute-start.57
  33.4 5.2 %collective-permute-done.55.refs_2_ = bf16[144,768]{1,0:T(8,128)(2,1)S(1)} collective-permute-done((bf16[144,768]{1,0:T(8,128)(2,1)S(1)}, bf16[144,768]{1,0:T(8,128)(2,1)S(1)}, u32[]{:S(2)}, u32[]{:S(2)}) %collective-permute-start.55) | collective-permute-done | bytes 221216 | tf_op jit(solution)/shard_map/ppermute | solution.py:19
  38.7 3.2 %collective-permute-done.56.refs_3_ = bf16[144,768]{1,0:T(8,128)(2,1)S(1)} collective-permute-done((bf16[144,768]{1,0:T(8,128)(2,1)S(1)}, bf16[144,768]{1,0:T(8,128)(2,1)S(1)}, u32[]{:S(2)}, u32[]{:S(2)}) %collective-permute-start.56) | collective-permute-done | bytes 221216 | tf_op jit(solution)/shard_map/ppermute | solution.py:19
  41.9 2.5 %collective-permute-start.59 = (bf16[144,768]{1,0:T(8,128)(2,1)S(1)}, bf16[144,768]{1,0:T(8,128)(2,1)S(1)}, u32[]{:S(2)}, u32[]{:S(2)}) collective-permute-start(bf16[144,768]{1,0:T(8,128)(2,1)S(1)} %get-tuple-element.223), channel_id=1, source_target_pairs={{0,6},{1,7},{2,4},{3,5},{4,2},{5,3},{6,0},{7,1},{8,14},{9,15},{10,... | collective-permute-start | bytes 663560 | tf_op jit(solution)/shard_map/ppermute | solution.py:19
  45.1 6.8 %own_slots.1.held_in = bf16[7168,768]{1,0:T(8,128)(2,1)} custom-call(s32[128,256]{1,0:T(8,128)S(1)} %get-tuple-element.230.pos_ref.pos, bf16[4096,768]{1,0:T(8,128)(2,1)} %x_ref.5), custom_call_target="tpu_custom_call" | custom-call | flops 2000000000 | bytes 13000000 | tf_op jit(solution)/shard_map/own_slots/pallas_call | solution.py:387
  52.0 3.9 %collective-permute-done.60.refs_7_ = bf16[144,768]{1,0:T(8,128)(2,1)S(1)} collective-permute-done((bf16[144,768]{1,0:T(8,128)(2,1)S(1)}, bf16[144,768]{1,0:T(8,128)(2,1)S(1)}, u32[]{:S(2)}, u32[]{:S(2)}) %collective-permute-start.60) | collective-permute-done | bytes 221216 | tf_op jit(solution)/shard_map/ppermute | solution.py:19
  57.4 51.0 %conditional.1 = (bf16[1024,768]{1,0:T(8,128)(2,1)}, bf16[528,768]{1,0:T(8,128)(2,1)}, s32[8,256]{1,0:T(8,128)}) conditional(s32[]{:T(128)} %bitcast.2, (bf16[528,768]{1,0:T(8,128)(2,1)}, s32[8,256]{1,0:T(8,128)S(1)}) %tuple.84, (bf16[1024,768]{1,0:T(8,128)(2,1)S(1)}, bf16[528,768]{1,0:T(8,128)(2,1)}, ...), branch_computations={%region_0.1_spmd, %region_1.2_spmd, %region_2.3_spmd, %region_3.4_... | conditional | bytes 15171730 | solution.py:677
  58.3 2.3 %collective-permute-start.34 = (s32[8,256]{1,0:T(8,128)S(1)}, s32[8,256]{1,0:T(8,128)}, u32[]{:S(2)}, u32[]{:S(2)}) collective-permute-start(s32[8,256]{1,0:T(8,128)S(1)} %get-tuple-element.134), channel_id=1, source_target_pairs={{0,16},{1,17},{2,18},{3,19},{4,20},{5,21},{6,22},{7,23},{8,24},{9,... | collective-permute-start | bytes 24584 | tf_op jit(solution)/shard_map/cond/branch_11_fun/ppermute | solution.py:19
  60.6 46.7 %collective-permute-done.32 = bf16[704,768]{1,0:T(8,128)(2,1)S(1)} collective-permute-done((bf16[704,768]{1,0:T(8,128)(2,1)S(1)}, bf16[704,768]{1,0:T(8,128)(2,1)S(1)}, u32[]{:S(2)}, u32[]{:S(2)}) %collective-permute-start.32) | collective-permute-done | bytes 1081376 | tf_op jit(solution)/shard_map/cond/branch_11_fun/ppermute | solution.py:19
  107.2 1.2 pad.55
  108.5 2.1 %part_pack.1 = (bf16[128,768]{1,0:T(8,128)(2,1)S(1)}, bf16[128,768]{1,0:T(8,128)(2,1)S(1)}, bf16[128,768]{1,0:T(8,128)(2,1)S(1)}, bf16[128,768]{1,0:T(8,128)(2,1...) custom-call(s32[8,128]{1,0:T(8,128)S(1)} %get-tuple-element.225.begi, ...), custom_call_target="tpu_custom_call" | custom-call | bytes 3000000 | tf_op jit(solution)/shard_map/part_pack/pallas_call | solution.py:298
  110.7 1.4 collective-permute-done.62.refs_1_
  114.2 1.5 collective-permute-start.64
  115.7 2.3 %collective-permute-done.64 = f32[8,768]{1,0:T(8,128)S(1)} collective-permute-done((f32[8,768]{1,0:T(8,128)S(1)}, f32[8,768]{1,0:T(8,128)S(1)}, u32[]{:S(2)}, u32[]{:S(2)}) %collective-permute-start.64) | collective-permute-done | bytes 24608 | tf_op jit(solution)/shard_map/ppermute | solution.py:19
  118.0 1.5 collective-permute-start.65
  119.5 1.5 %collective-permute-start.67 = (bf16[128,768]{1,0:T(8,128)(2,1)S(1)}, bf16[128,768]{1,0:T(8,128)(2,1)S(1)}, u32[]{:S(2)}, u32[]{:S(2)}) collective-permute-start(bf16[128,768]{1,0:T(8,128)(2,1)S(1)} %get-tuple-element.251), channel_id=1, source_target_pairs={{0,2},{1,3},{2,0},{3,1},{4,6},{5,7},{6,4},{7,5},{8,10},{9,11},{10,... | collective-permute-start | bytes 589832 | tf_op jit(solution)/shard_map/ppermute | solution.py:19
  121.9 1.2 collective-permute-start.70
  123.0 5.8 %own_margins.1 = (f32[6,768]{1,0:T(8,128)}, bf16[16,768]{1,0:T(8,128)(2,1)S(1)}, bf16[768,128]{1,0:T(8,128)(2,1)S(1)}, f32[8,128]{1,0:T(8,128)S(1)}, f32[48,128]{1,0:T(8,128)}, /*index=5*/f32[56,128]{1,0:T(8,128)}) custom-call(s32[2]{0:T(128)S(1)} %pad_add_fusion.here, f32[8,768]{1,0:T(8,128)S(1)} %add.43.total, s32[2,4096]{1,0:T(2,128)S(1)} %copy-done.1, ...), custom_call_target="tpu_custom_call" | custom-call | flops 2000000000 | bytes 7000000 | tf_op jit(solution)/shard_map/own_margins/pallas_call | solution.py:443
  128.8 1.5 %collective-permute-start.71 = (bf16[128,768]{1,0:T(8,128)(2,1)S(1)}, bf16[128,768]{1,0:T(8,128)(2,1)S(1)}, u32[]{:S(2)}, u32[]{:S(2)}) collective-permute-start(bf16[128,768]{1,0:T(8,128)(2,1)S(1)} %get-tuple-element.255), channel_id=1, source_target_pairs={{0,6},{1,7},{2,4},{3,5},{4,2},{5,3},{6,0},{7,1},{8,14},{9,15},{10,... | collective-permute-start | bytes 589832 | tf_op jit(solution)/shard_map/ppermute | solution.py:19
  130.3 1.2 collective-permute-start.72
  131.6 4.2 %second_slots.1 = (bf16[7168,768]{1,0:T(8,128)(2,1)}, f32[56,128]{1,0:T(8,128)}, f32[16,128]{1,0:T(8,128)S(1)}, f32[16,128]{1,0:T(8,128)S(1)}, s32[8,128]{1,0:T(8,128)S(1)}, /*index=5*/s32[8,2048]{1,0:T(8,128)S(1)}) custom-call(bf16[16,768]{1,0:T(8,128)(2,1)S(1)} %get-tuple-element.238.centres, ...), custom_call_target="tpu_custom_call", output_to_operand_aliasing={{0}: (7, {}), {1}: (8, {})} | custom-call | flops 3000000000 | bytes 6000000 | tf_op jit(solution)/shard_map/second_slots/pallas_call | solution.py:519
  135.7 1.7 %collective-permute-done.71.refs_6_ = bf16[128,768]{1,0:T(8,128)(2,1)S(1)} collective-permute-done((bf16[128,768]{1,0:T(8,128)(2,1)S(1)}, bf16[128,768]{1,0:T(8,128)(2,1)S(1)}, u32[]{:S(2)}, u32[]{:S(2)}) %collective-permute-start.71) | collective-permute-done | bytes 196640 | tf_op jit(solution)/shard_map/ppermute | solution.py:19
  137.5 3.3 %collective-permute-done.72.refs_7_ = bf16[128,768]{1,0:T(8,128)(2,1)S(1)} collective-permute-done((bf16[128,768]{1,0:T(8,128)(2,1)S(1)}, bf16[128,768]{1,0:T(8,128)(2,1)S(1)}, u32[]{:S(2)}, u32[]{:S(2)}) %collective-permute-start.72) | collective-permute-done | bytes 196640 | tf_op jit(solution)/shard_map/ppermute | solution.py:19
  140.8 2.3 %collective-permute-done.66.middle = bf16[512,768]{1,0:T(8,128)(2,1)S(1)} collective-permute-done((bf16[512,768]{1,0:T(8,128)(2,1)S(1)}, bf16[512,768]{1,0:T(8,128)(2,1)S(1)}, u32[]{:S(2)}, u32[]{:S(2)}) %collective-permute-start.66) | collective-permute-done | bytes 786464 | tf_op jit(solution)/shard_map/ppermute | solution.py:19
  143.0 7.7 %first_slots.1 = (bf16[7168,768]{1,0:T(8,128)(2,1)}, f32[48,128]{1,0:T(8,128)}, f32[56,128]{1,0:T(8,128)}) custom-call(s32[8,128]{1,0:T(8,128)S(1)} %get-tuple-element.243.start, bf16[768,128]{1,0:T(8,128)(2,1)S(1)} %get-tuple-element.244.turned, ...), custom_call_target="tpu_custom_call", output_to_operand_aliasing={{0}: (16, {}), {1}: (17, {}), {2}: (18, {})} | custom-call | flops 3000000000 | bytes 7000000 | tf_op jit(solution)/shard_map/first_slots/pallas_call | solution.py:615
  (43 shorter events, 8.0 us)
Async XLA Ops:
  0.7 0.8 copy-start
  2.4 16.5 %collective-permute-start.52 = (s32[8,128]{1,0:T(8,128)S(1)}, s32[8,128]{1,0:T(8,128)S(1)}, u32[]{:S(2)}, u32[]{:S(2)}) collective-permute-start(s32[8,128]{1,0:T(8,128)S(1)} %get-tuple-element.214.own), channel_id=1, source_target_pairs={{0,24},{1,25},{2,26},{3,27},{4,28},{5,29},{6,30},{7,31},{8,16},{9,... | collective-permute-start | bytes 12296 | tf_op jit(solution)/shard_map/ppermute | solution.py:19
  7.5 11.4 %collective-permute-start.51 = (s32[8,128]{1,0:T(8,128)S(1)}, s32[8,128]{1,0:T(8,128)S(1)}, u32[]{:S(2)}, u32[]{:S(2)}) collective-permute-start(s32[8,128]{1,0:T(8,128)S(1)} %get-tuple-element.214.own), channel_id=1, source_target_pairs={{0,16},{1,17},{2,18},{3,19},{4,20},{5,21},{6,22},{7,23},{8,24},{9,... | collective-permute-start | bytes 12296 | tf_op jit(solution)/shard_map/ppermute | solution.py:19
  7.5 11.4 %collective-permute-start.50 = (s32[8,128]{1,0:T(8,128)S(1)}, s32[8,128]{1,0:T(8,128)S(1)}, u32[]{:S(2)}, u32[]{:S(2)}) collective-permute-start(s32[8,128]{1,0:T(8,128)S(1)} %get-tuple-element.214.own), channel_id=1, source_target_pairs={{0,8},{1,9},{2,10},{3,11},{4,12},{5,13},{6,14},{7,15},{8,0},{9,1},... | collective-permute-start | bytes 12296 | tf_op jit(solution)/shard_map/ppermute | solution.py:19
  16.6 40.9 %collective-permute-start.61 = (bf16[528,768]{1,0:T(8,128)(2,1)S(1)}, bf16[528,768]{1,0:T(8,128)(2,1)}, u32[]{:S(2)}, u32[]{:S(2)}) collective-permute-start(bf16[528,768]{1,0:T(8,128)(2,1)S(1)} %get-tuple-element.212.extra.own), channel_id=1, source_target_pairs={{0,16},{1,17},{2,18},{3,19},{4,20},{5,21},{6,22},{7,23},{8,24},{9,... | collective-permute-start | bytes 2433032 | tf_op jit(solution)/shard_map/ppermute | solution.py:19
  22.0 9.9 %collective-permute-start.54 = (bf16[144,768]{1,0:T(8,128)(2,1)S(1)}, bf16[144,768]{1,0:T(8,128)(2,1)S(1)}, u32[]{:S(2)}, u32[]{:S(2)}) collective-permute-start(bf16[144,768]{1,0:T(8,128)(2,1)S(1)} %get-tuple-element.218), channel_id=1, source_target_pairs={{0,1},{1,0},{2,3},{3,2},{4,5},{5,4},{6,7},{7,6},{8,9},{9,8},{10,11... | collective-permute-start | bytes 663560 | tf_op jit(solution)/shard_map/ppermute | solution.py:19
  28.3 82.4 %collective-permute-start.53 = (bf16[528,768]{1,0:T(8,128)(2,1)S(1)}, bf16[528,768]{1,0:T(8,128)(2,1)S(1)}, u32[]{:S(2)}, u32[]{:S(2)}) collective-permute-start(bf16[528,768]{1,0:T(8,128)(2,1)S(1)} %get-tuple-element.217), channel_id=1, source_target_pairs={{0,8},{1,9},{2,10},{3,11},{4,12},{5,13},{6,14},{7,15},{8,0},{9,1},... | collective-permute-start | bytes 2433032 | tf_op jit(solution)/shard_map/ppermute | solution.py:19
  30.4 8.3 %collective-permute-start.55 = (bf16[144,768]{1,0:T(8,128)(2,1)S(1)}, bf16[144,768]{1,0:T(8,128)(2,1)S(1)}, u32[]{:S(2)}, u32[]{:S(2)}) collective-permute-start(bf16[144,768]{1,0:T(8,128)(2,1)S(1)} %get-tuple-element.219), channel_id=1, source_target_pairs={{0,2},{1,3},{2,0},{3,1},{4,6},{5,7},{6,4},{7,5},{8,10},{9,11},{10,... | collective-permute-start | bytes 663560 | tf_op jit(solution)/shard_map/ppermute | solution.py:19
  31.9 10.0 %collective-permute-start.56 = (bf16[144,768]{1,0:T(8,128)(2,1)S(1)}, bf16[144,768]{1,0:T(8,128)(2,1)S(1)}, u32[]{:S(2)}, u32[]{:S(2)}) collective-permute-start(bf16[144,768]{1,0:T(8,128)(2,1)S(1)} %get-tuple-element.220), channel_id=1, source_target_pairs={{0,3},{1,2},{2,1},{3,0},{4,7},{5,6},{6,5},{7,4},{8,11},{9,10},{10,... | collective-permute-start | bytes 663560 | tf_op jit(solution)/shard_map/ppermute | solution.py:19
  31.9 12.4 %collective-permute-start.57 = (bf16[144,768]{1,0:T(8,128)(2,1)S(1)}, bf16[144,768]{1,0:T(8,128)(2,1)S(1)}, u32[]{:S(2)}, u32[]{:S(2)}) collective-permute-start(bf16[144,768]{1,0:T(8,128)(2,1)S(1)} %get-tuple-element.221), channel_id=1, source_target_pairs={{0,4},{1,5},{2,6},{3,7},{4,0},{5,1},{6,2},{7,3},{8,12},{9,13},{10,... | collective-permute-start | bytes 663560 | tf_op jit(solution)/shard_map/ppermute | solution.py:19
  38.6 13.3 %collective-permute-start.58 = (bf16[144,768]{1,0:T(8,128)(2,1)S(1)}, bf16[144,768]{1,0:T(8,128)(2,1)S(1)}, u32[]{:S(2)}, u32[]{:S(2)}) collective-permute-start(bf16[144,768]{1,0:T(8,128)(2,1)S(1)} %get-tuple-element.222), channel_id=1, source_target_pairs={{0,5},{1,4},{2,7},{3,6},{4,1},{5,0},{6,3},{7,2},{8,13},{9,12},{10,... | collective-permute-start | bytes 663560 | tf_op jit(solution)/shard_map/ppermute | solution.py:19
  41.9 10.1 %collective-permute-start.59 = (bf16[144,768]{1,0:T(8,128)(2,1)S(1)}, bf16[144,768]{1,0:T(8,128)(2,1)S(1)}, u32[]{:S(2)}, u32[]{:S(2)}) collective-permute-start(bf16[144,768]{1,0:T(8,128)(2,1)S(1)} %get-tuple-element.223), channel_id=1, source_target_pairs={{0,6},{1,7},{2,4},{3,5},{4,2},{5,3},{6,0},{7,1},{8,14},{9,15},{10,... | collective-permute-start | bytes 663560 | tf_op jit(solution)/shard_map/ppermute | solution.py:19
  44.4 11.5 %collective-permute-start.60 = (bf16[144,768]{1,0:T(8,128)(2,1)S(1)}, bf16[144,768]{1,0:T(8,128)(2,1)S(1)}, u32[]{:S(2)}, u32[]{:S(2)}) collective-permute-start(bf16[144,768]{1,0:T(8,128)(2,1)S(1)} %get-tuple-element.224), channel_id=1, source_target_pairs={{0,7},{1,6},{2,5},{3,4},{4,3},{5,2},{6,1},{7,0},{8,15},{9,14},{10,... | collective-permute-start | bytes 663560 | tf_op jit(solution)/shard_map/ppermute | solution.py:19
  57.6 49.6 %collective-permute-start.32 = (bf16[704,768]{1,0:T(8,128)(2,1)S(1)}, bf16[704,768]{1,0:T(8,128)(2,1)S(1)}, u32[]{:S(2)}, u32[]{:S(2)}) collective-permute-start(bf16[704,768]{1,0:T(8,128)(2,1)S(1)} %slice.42), channel_id=1, source_target_pairs={{0,16},{1,17},{2,18},{3,19},{4,20},{5,21},{6,22},{7,23},{8,24},{9,... | collective-permute-start | bytes 3244040 | tf_op jit(solution)/shard_map/cond/branch_11_fun/ppermute | solution.py:19
  57.6 50.8 %collective-permute-start.33 = (bf16[528,768]{1,0:T(8,128)(2,1)}, bf16[528,768]{1,0:T(8,128)(2,1)}, u32[]{:S(2)}, u32[]{:S(2)}) collective-permute-start(bf16[528,768]{1,0:T(8,128)(2,1)} %get-tuple-element.133), channel_id=1, source_target_pairs={{0,8},{1,9},{2,10},{3,11},{4,12},{5,13},{6,14},{7,15},{8,0},{9,1},... | collective-permute-start | bytes 2433032 | tf_op jit(solution)/shard_map/cond/branch_11_fun/ppermute | solution.py:19
  58.3 50.2 %collective-permute-start.34 = (s32[8,256]{1,0:T(8,128)S(1)}, s32[8,256]{1,0:T(8,128)}, u32[]{:S(2)}, u32[]{:S(2)}) collective-permute-start(s32[8,256]{1,0:T(8,128)S(1)} %get-tuple-element.134), channel_id=1, source_target_pairs={{0,16},{1,17},{2,18},{3,19},{4,20},{5,21},{6,22},{7,23},{8,24},{9,... | collective-permute-start | bytes 24584 | tf_op jit(solution)/shard_map/cond/branch_11_fun/ppermute | solution.py:19
  108.5 34.6 %collective-permute-start.66 = (bf16[512,768]{1,0:T(8,128)(2,1)S(1)}, bf16[512,768]{1,0:T(8,128)(2,1)S(1)}, u32[]{:S(2)}, u32[]{:S(2)}) collective-permute-start(bf16[512,768]{1,0:T(8,128)(2,1)S(1)} %get-tuple-element.248), channel_id=1, source_target_pairs={{0,16},{1,17},{2,18},{3,19},{4,20},{5,21},{6,22},{7,23},{8,24},{9,... | collective-permute-start | bytes 2359304 | tf_op jit(solution)/shard_map/ppermute | solution.py:19
  110.6 1.5 collective-permute-start.62
  112.1 10.9 %copy-start.1 = (s32[2,4096]{1,0:T(2,128)S(1)}, s32[2,4096]{1,0:T(2,128)}, u32[]{:S(2)}) copy-start(s32[2,4096]{1,0:T(2,128)} %labels.5) | copy-start | bytes 98308
  113.0 1.2 collective-permute-start.63
  114.2 3.8 %collective-permute-start.64 = (f32[8,768]{1,0:T(8,128)S(1)}, f32[8,768]{1,0:T(8,128)S(1)}, u32[]{:S(2)}, u32[]{:S(2)}) collective-permute-start(f32[8,768]{1,0:T(8,128)S(1)} %add.41), channel_id=1, source_target_pairs={{0,2},{1,3},{2,0},{3,1},{4,6},{5,7},{6,4},{7,5},{8,10},{9,11},{10,... | collective-permute-start | bytes 73736 | tf_op jit(solution)/shard_map/ppermute | solution.py:19
  118.0 3.8 %collective-permute-start.65 = (f32[8,768]{1,0:T(8,128)S(1)}, f32[8,768]{1,0:T(8,128)S(1)}, u32[]{:S(2)}, u32[]{:S(2)}) collective-permute-start(f32[8,768]{1,0:T(8,128)S(1)} %add.42), channel_id=1, source_target_pairs={{0,4},{1,5},{2,6},{3,7},{4,0},{5,1},{6,2},{7,3},{8,12},{9,13},{10,... | collective-permute-start | bytes 73736 | tf_op jit(solution)/shard_map/ppermute | solution.py:19
  119.5 9.3 %collective-permute-start.67 = (bf16[128,768]{1,0:T(8,128)(2,1)S(1)}, bf16[128,768]{1,0:T(8,128)(2,1)S(1)}, u32[]{:S(2)}, u32[]{:S(2)}) collective-permute-start(bf16[128,768]{1,0:T(8,128)(2,1)S(1)} %get-tuple-element.251), channel_id=1, source_target_pairs={{0,2},{1,3},{2,0},{3,1},{4,6},{5,7},{6,4},{7,5},{8,10},{9,11},{10,... | collective-permute-start | bytes 589832 | tf_op jit(solution)/shard_map/ppermute | solution.py:19
  121.0 9.3 %collective-permute-start.68 = (bf16[128,768]{1,0:T(8,128)(2,1)S(1)}, bf16[128,768]{1,0:T(8,128)(2,1)S(1)}, u32[]{:S(2)}, u32[]{:S(2)}) collective-permute-start(bf16[128,768]{1,0:T(8,128)(2,1)S(1)} %get-tuple-element.252), channel_id=1, source_target_pairs={{0,3},{1,2},{2,1},{3,0},{4,7},{5,6},{6,5},{7,4},{8,11},{9,10},{10,... | collective-permute-start | bytes 589832 | tf_op jit(solution)/shard_map/ppermute | solution.py:19
  121.0 14.7 %collective-permute-start.69 = (bf16[128,768]{1,0:T(8,128)(2,1)S(1)}, bf16[128,768]{1,0:T(8,128)(2,1)S(1)}, u32[]{:S(2)}, u32[]{:S(2)}) collective-permute-start(bf16[128,768]{1,0:T(8,128)(2,1)S(1)} %get-tuple-element.253), channel_id=1, source_target_pairs={{0,4},{1,5},{2,6},{3,7},{4,0},{5,1},{6,2},{7,3},{8,12},{9,13},{10,... | collective-permute-start | bytes 589832 | tf_op jit(solution)/shard_map/ppermute | solution.py:19
  121.9 13.9 %collective-permute-start.70 = (bf16[128,768]{1,0:T(8,128)(2,1)S(1)}, bf16[128,768]{1,0:T(8,128)(2,1)S(1)}, u32[]{:S(2)}, u32[]{:S(2)}) collective-permute-start(bf16[128,768]{1,0:T(8,128)(2,1)S(1)} %get-tuple-element.254), channel_id=1, source_target_pairs={{0,5},{1,4},{2,7},{3,6},{4,1},{5,0},{6,3},{7,2},{8,13},{9,12},{10,... | collective-permute-start | bytes 589832 | tf_op jit(solution)/shard_map/ppermute | solution.py:19
  128.8 8.7 %collective-permute-start.71 = (bf16[128,768]{1,0:T(8,128)(2,1)S(1)}, bf16[128,768]{1,0:T(8,128)(2,1)S(1)}, u32[]{:S(2)}, u32[]{:S(2)}) collective-permute-start(bf16[128,768]{1,0:T(8,128)(2,1)S(1)} %get-tuple-element.255), channel_id=1, source_target_pairs={{0,6},{1,7},{2,4},{3,5},{4,2},{5,3},{6,0},{7,1},{8,14},{9,15},{10,... | collective-permute-start | bytes 589832 | tf_op jit(solution)/shard_map/ppermute | solution.py:19
  130.3 10.4 %collective-permute-start.72 = (bf16[128,768]{1,0:T(8,128)(2,1)S(1)}, bf16[128,768]{1,0:T(8,128)(2,1)S(1)}, u32[]{:S(2)}, u32[]{:S(2)}) collective-permute-start(bf16[128,768]{1,0:T(8,128)(2,1)S(1)} %get-tuple-element.256), channel_id=1, source_target_pairs={{0,7},{1,6},{2,5},{3,4},{4,3},{5,2},{6,1},{7,0},{8,15},{9,14},{10,... | collective-permute-start | bytes 589832 | tf_op jit(solution)/shard_map/ppermute | solution.py:19
